TPU v7x, 32 devices: a whole 2x2x4 slice. The times are simulated.
32 devices in a mesh: dp: 8 (over z, y), tensor: 4 (over x, core).
Axes of the slice: x: 2, y: 2, z: 4, core: 2. Of those that a mesh axis runs over, the one named last changes fastest.
Arguments:
- tokens_in: bfloat16 [16384, 768], P(('dp', 'tensor')), may hold values from -6 to 6
- carried_logits: float32 [16384, 12], P(('dp', 'tensor')), may hold values from -3 to 3
- cotangent: bfloat16 [16384, 768], P(('dp', 'tensor')), may hold values from -6 to 6
- segment_ids: int32 [16384], P('dp'), may hold values from 0 to 12, as said below
- parent_ids: int32 [16384], P('dp'), may hold values from 0 to 4, as said below
- routes: int32 [16384, 2], P('dp'), may hold values from 0 to 11, all different within a row; in each aligned block of 2048 rows (0 to 2047, 2048 to 4095, ...) at most 512 rows name the same one
- attention_gain: float32 [768], replicated, may hold values from 0.5 to 1.5
- head_weight: float32 [3, 768, 768], P(None, 'dp', 'tensor'), may hold values from -0.21875 to 0.21875
- output_weight: float32 [768, 768], P('tensor', 'dp'), may hold values from -2.5 to 2.5
- expert_gain: float32 [768], replicated, may hold values from 0.5 to 1.5
- router_weight: float32 [768, 12], replicated, may hold values from -0.15625 to 0.15625
- carry_weight: float32 [12, 12], replicated, may hold values from -1.25 to 1.25
- constant_gate: float32 [768, 4], replicated, may hold values from -0.21875 to 0.21875
- constant_vector: float32 [2, 768], replicated, may hold values from -6 to 6
- expert_first: float32 [8, 2, 768, 2048], P(None, None, 'dp', 'tensor'), may hold values from -0.21875 to 0.21875
- expert_second: float32 [8, 2048, 768], P(None, 'tensor', 'dp'), may hold values from -0.25 to 0.25
Outputs:
- output: bfloat16 [16384, 768], P(('dp', 'tensor'))
- grad_tokens: float32 [16384, 768], P(('dp', 'tensor'))
- grad_carried: float32 [16384, 12], P(('dp', 'tensor'))
- grad_attention_gain: float32 [768], replicated
- grad_head_weight: float32 [3, 768, 768], P(None, 'dp', 'tensor')
- grad_output_weight: float32 [768, 768], P('tensor', 'dp')
- grad_expert_gain: float32 [768], replicated
- grad_router_weight: float32 [768, 12], replicated
- grad_carry_weight: float32 [12, 12], replicated
- grad_constant_gate: float32 [768, 4], replicated
- grad_constant_vector: float32 [2, 768], replicated
- grad_expert_first: float32 [8, 2, 768, 2048], P(None, None, 'dp', 'tensor')
- grad_expert_second: float32 [8, 2048, 768], P(None, 'tensor', 'dp')
Inputs may be any that keep to these rules, and one draw needn't show every extreme that they name: `segment_ids`: in each tree (aligned blocks of 2048 tokens) the segments come in order: 0 is the trunk (the first 768 tokens), 1 to 4 are branches, the rest leaves; every segment holds a token. `parent_ids`: the parent of the trunk and of every branch is 0; each branch is the parent of two leaves. `routes`: A token's two experts differ; in each tree no expert is named by more than 512 tokens, a bound that some block reaches.
All inputs are finite; a program needn't handle non-finite values.
Results may differ from a plain program's by a relative error of at most 0.017.
Values may be sent and summed in bfloat16 or wider, within the bound.
A program may use at most 256 MiB of HBM per device.

v0:
```python
from functools import partial

import jax
import jax.numpy as jnp
from jax import lax
from jax.sharding import PartitionSpec as P

HEAD = 64
NF = 8
NSEG = 13
NE = 12


epsilon = 1e-06
HIGHEST = lax.Precision.HIGHEST


def normed(values, gain_vector):
    return (
        values
        * lax.rsqrt(jnp.mean(values * values, axis=-1, keepdims=True) + epsilon)
        * gain_vector
    )


def tree_positions(segment, parent):
    token_count = segment.shape[0]
    labels = jnp.arange(NSEG, dtype=jnp.int32)
    own_hot = (segment[:, None] == labels[None, :]).astype(jnp.int32)
    parent_hot = (parent[:, None] == labels[None, :]).astype(jnp.int32)
    lengths = jnp.sum(own_hot, axis=0)
    starts = jnp.cumsum(lengths) - lengths
    own_start = jnp.sum(own_hot * starts[None, :], axis=1)
    parent_length = jnp.sum(parent_hot * lengths[None, :], axis=1)
    position_index = jnp.arange(token_count, dtype=jnp.int32)
    shifted = (
        position_index
        - own_start
        + jnp.where(segment > 0, lengths[0], 0)
        + jnp.where(parent > 0, parent_length, 0)
    )
    return shifted


def rotary_tables(segment, parent):
    angle_rate = 10000.0 ** (-2.0 * jnp.arange(HEAD // 2, dtype=jnp.float32) / HEAD)
    angles = tree_positions(segment, parent).astype(jnp.float32)[:, None] * angle_rate[None, :]
    return (jnp.cos(angles)[:, None, :], jnp.sin(angles)[:, None, :])


def rotary(values, cosine, sine_part):
    half_size = values.shape[-1] // 2
    first_half = values[..., :half_size]
    second_half = values[..., half_size:]
    return jnp.concatenate(
        [
            first_half * cosine - second_half * sine_part,
            second_half * cosine + first_half * sine_part,
        ],
        axis=-1,
    )


def visibility(row_index, row_segment, row_parent, segment):
    columns = jnp.arange(segment.shape[0], dtype=jnp.int32)
    related = (
        (segment[None, :] == row_segment[:, None])
        | (segment[None, :] == row_parent[:, None])
        | (segment[None, :] == 0)
    )
    return (columns[None, :] <= row_index[:, None]) & related


def router_local(
    hidden,
    gain_vector,
    carried,
    router_weight,
    carry_weight,
    constant_gate,
    constant_vector,
    routes,
):
    normed_two = normed(hidden, gain_vector)
    logits = jnp.dot(normed_two, router_weight, precision=HIGHEST) + jnp.dot(
        carried, carry_weight, precision=HIGHEST
    )
    picked = (routes[:, :, None] == jnp.arange(NE, dtype=jnp.int32)[None, None, :]).astype(
        jnp.float32
    )
    chosen = jnp.einsum("tkn,tn->tk", picked, logits, precision=HIGHEST)
    gate_values = jax.nn.softmax(chosen, axis=-1)
    mixture = jax.nn.softmax(
        jnp.dot(normed_two, constant_gate, precision=HIGHEST).reshape(-1, 2, 2), axis=-1
    )
    copy_weight = jnp.sum(gate_values * (routes == NF + 1).astype(jnp.float32), axis=1)
    first_weight = jnp.sum(gate_values * (routes == NF + 2).astype(jnp.float32), axis=1)
    second_weight = jnp.sum(gate_values * (routes == NF + 3).astype(jnp.float32), axis=1)
    local_sum = copy_weight[:, None] * normed_two
    local_sum = local_sum + first_weight[:, None] * (
        mixture[:, 0, 0:1] * normed_two + mixture[:, 0, 1:2] * constant_vector[0][None, :]
    )
    local_sum = local_sum + second_weight[:, None] * (
        mixture[:, 1, 0:1] * normed_two + mixture[:, 1, 1:2] * constant_vector[1][None, :]
    )
    expert_gates = gate_values * (routes < NF).astype(jnp.float32)
    return (normed_two, expert_gates, local_sum)


def dispatch(routes, capacity):
    flat_routes = routes.reshape(-1)
    one_hot = (flat_routes[:, None] == jnp.arange(NE, dtype=jnp.int32)[None, :]).astype(jnp.int32)
    before = jnp.cumsum(one_hot, axis=0) - one_hot
    slot_index = jnp.sum(before * one_hot, axis=1)
    slot_place = jnp.where(flat_routes < NF, flat_routes * capacity + slot_index, NF * capacity)
    anchor = jnp.arange(flat_routes.shape[0], dtype=jnp.int32)
    return (
        jnp.full((NF * capacity,), flat_routes.shape[0], jnp.int32)
        .at[slot_place]
        .set(anchor, mode="drop")
    )


def per_device(
    tokens_in,
    carried_logits,
    cotangent,
    segment_ids,
    parent_ids,
    routes,
    attention_gain,
    head_weight,
    output_weight,
    expert_gain,
    router_weight,
    carry_weight,
    constant_gate,
    constant_vector,
    expert_first,
    expert_second,
):
    row_count = tokens_in.shape[0]
    width = tokens_in.shape[1]
    tree_len = segment_ids.shape[0]
    capacity = tree_len // 4
    local_heads = head_weight.shape[2] // HEAD
    head_width = head_weight.shape[2]
    block_rows = min(512, tree_len)
    block_count = tree_len // block_rows
    score_scale = HEAD ** (-0.5)
    local_routes = lax.dynamic_slice_in_dim(
        routes, lax.axis_index("tensor") * row_count, row_count, 0
    )
    head_low = head_weight.astype(jnp.bfloat16)
    output_low = output_weight.astype(jnp.bfloat16)
    first_low = expert_first.astype(jnp.bfloat16)
    second_low = expert_second.astype(jnp.bfloat16)
    head_full, output_full = (
        lax.all_gather(head_low, "dp", axis=1, tiled=True),
        lax.all_gather(output_low, "dp", axis=1, tiled=True),
    )
    token_values = tokens_in.astype(jnp.float32)
    normed_one = normed(token_values, attention_gain).astype(jnp.bfloat16)
    gathered_one = lax.all_gather(normed_one, "tensor", axis=0, tiled=True)
    projected = jnp.einsum(
        "td,sdf->stf", gathered_one, head_full, preferred_element_type=jnp.float32
    )
    cosine, sine_part = rotary_tables(segment_ids, parent_ids)
    queries = rotary(projected[0].reshape(tree_len, local_heads, HEAD), cosine, sine_part).astype(
        jnp.bfloat16
    )
    keys_all = rotary(projected[1].reshape(tree_len, local_heads, HEAD), cosine, sine_part).astype(
        jnp.bfloat16
    )
    values_all = projected[2].reshape(tree_len, local_heads, HEAD).astype(jnp.bfloat16)
    row_index = jnp.arange(tree_len, dtype=jnp.int32).reshape(block_count, block_rows)
    segment_blocks = segment_ids.reshape(block_count, block_rows)
    parent_blocks = parent_ids.reshape(block_count, block_rows)
    query_blocks = queries.reshape(block_count, block_rows, local_heads, HEAD)

    def block_scores(query_block, visible):
        scores = (
            jnp.einsum("qhe,khe->hqk", query_block, keys_all, preferred_element_type=jnp.float32)
            * score_scale
        )
        return jnp.where(visible[None], scores, -1e30)

    def forward_block(block_args):
        query_block, index_block, segment_block, parent_block = block_args
        visible = visibility(index_block, segment_block, parent_block, segment_ids)
        scores = block_scores(query_block, visible)
        row_max = jnp.max(scores, axis=-1, keepdims=True)
        exponent = jnp.exp(scores - row_max)
        row_total = jnp.sum(exponent, axis=-1, keepdims=True)
        probs_low = (exponent / row_total).astype(jnp.bfloat16)
        mixed_out = jnp.einsum(
            "hqk,khe->qhe", probs_low, values_all, preferred_element_type=jnp.float32
        )
        return (mixed_out, (row_max + jnp.log(row_total))[..., 0])

    mixed_out, log_total = lax.map(
        forward_block, (query_blocks, row_index, segment_blocks, parent_blocks)
    )
    attended = mixed_out.reshape(tree_len, head_width).astype(jnp.bfloat16)
    attention_part = jnp.dot(attended, output_full, preferred_element_type=jnp.float32)
    attention_total = lax.psum_scatter(attention_part, "tensor", scatter_dimension=0, tiled=True)
    hidden = token_values + attention_total
    router_fn = partial(router_local, routes=local_routes)
    (normed_two, expert_gates, local_sum), pull_router = jax.vjp(
        router_fn,
        hidden,
        expert_gain,
        carried_logits,
        router_weight,
        carry_weight,
        constant_gate,
        constant_vector,
    )
    gathered_two, gate_two = (
        lax.all_gather(normed_two.astype(jnp.bfloat16), "tensor", axis=0, tiled=True),
        lax.all_gather(expert_gates.astype(jnp.bfloat16), "tensor", axis=0, tiled=True),
    )
    first_full, second_full = (
        lax.all_gather(first_low, "dp", axis=2, tiled=True),
        lax.all_gather(second_low, "dp", axis=2, tiled=True),
    )
    source = dispatch(routes, capacity)
    filled = source < 2 * tree_len
    token_index = jnp.where(filled, source // 2, 0)
    safe_source = jnp.minimum(source, 2 * tree_len - 1)
    slot_gate = jnp.where(filled, gate_two.reshape(-1)[safe_source].astype(jnp.float32), 0.0)
    expert_rows = gathered_two[token_index].reshape(NF, capacity, width)
    inner_out = jnp.einsum(
        "ecd,esdf->escf", expert_rows, first_full, preferred_element_type=jnp.float32
    )
    gate_part = inner_out[:, 0]
    up_part = inner_out[:, 1]
    activated = (jax.nn.silu(gate_part) * up_part).astype(jnp.bfloat16)
    expert_out = jnp.einsum(
        "ecf,efd->ecd", activated, second_full, preferred_element_type=jnp.float32
    ).reshape(NF * capacity, width)
    expert_partial = (
        jnp.zeros((tree_len, width), jnp.float32)
        .at[token_index]
        .add(expert_out * slot_gate[:, None])
    )
    expert_total = lax.psum_scatter(
        expert_partial.astype(jnp.bfloat16), "tensor", scatter_dimension=0, tiled=True
    ).astype(jnp.float32)
    output = (hidden + local_sum + expert_total).astype(jnp.bfloat16)
    head_back, output_back, first_back, second_back = (
        lax.all_gather(head_low, "dp", axis=1, tiled=True),
        lax.all_gather(output_low, "dp", axis=1, tiled=True),
        lax.all_gather(first_low, "dp", axis=2, tiled=True),
        lax.all_gather(second_low, "dp", axis=2, tiled=True),
    )
    grad_values_out = cotangent.astype(jnp.float32)
    grad_rows = lax.all_gather(cotangent, "tensor", axis=0, tiled=True)
    slot_grad = grad_rows[token_index].astype(jnp.float32)
    grad_outer = (slot_grad * slot_gate[:, None]).astype(jnp.bfloat16).reshape(NF, capacity, width)
    slot_gate_grad = jnp.sum(slot_grad * expert_out, axis=1)
    gate_target = jnp.where(filled, source, 2 * tree_len)
    gate_grad = (
        jnp.zeros((2 * tree_len,), jnp.float32)
        .at[gate_target]
        .add(slot_gate_grad, mode="drop")
        .reshape(tree_len, 2)
    )
    grad_act = jnp.einsum(
        "ecd,efd->ecf", grad_outer, second_back, preferred_element_type=jnp.float32
    )
    grad_second = jnp.einsum(
        "ecf,ecd->efd", activated, grad_outer, preferred_element_type=jnp.float32
    )
    sigmoid_gate = jax.nn.sigmoid(gate_part)
    grad_gate = grad_act * up_part * sigmoid_gate * (1.0 + gate_part * (1.0 - sigmoid_gate))
    grad_up = grad_act * gate_part * sigmoid_gate
    grad_inner = jnp.stack([grad_gate, grad_up], axis=1).astype(jnp.bfloat16)
    grad_first = jnp.einsum(
        "ecd,escf->esdf", expert_rows, grad_inner, preferred_element_type=jnp.float32
    )
    grad_slot_rows = jnp.einsum(
        "escf,esdf->ecd", grad_inner, first_back, preferred_element_type=jnp.float32
    ).reshape(NF * capacity, width)
    grad_gathered = jnp.zeros((tree_len, width), jnp.float32).at[token_index].add(grad_slot_rows)
    grad_normed_two, grad_gate_two = (
        lax.psum_scatter(grad_gathered, "tensor", scatter_dimension=0, tiled=True),
        lax.psum_scatter(gate_grad, "tensor", scatter_dimension=0, tiled=True),
    )
    grad_first_own, grad_second_own = (
        lax.psum_scatter(grad_first, "dp", scatter_dimension=2, tiled=True),
        lax.psum_scatter(grad_second, "dp", scatter_dimension=2, tiled=True),
    )
    (
        grad_hidden_local,
        grad_expert_gain,
        grad_carried,
        grad_router,
        grad_carry,
        grad_constant_gate,
        grad_constant_vector,
    ) = pull_router((grad_normed_two, grad_gate_two, grad_values_out))
    grad_hidden = grad_values_out + grad_hidden_local
    grad_branch = lax.all_gather(grad_hidden.astype(jnp.bfloat16), "tensor", axis=0, tiled=True)
    grad_output_weight = jnp.einsum(
        "tf,td->fd", attended, grad_branch, preferred_element_type=jnp.float32
    )
    grad_attended = jnp.einsum(
        "td,fd->tf", grad_branch, output_back, preferred_element_type=jnp.float32
    ).astype(jnp.bfloat16)
    grad_attended_blocks = grad_attended.reshape(block_count, block_rows, local_heads, HEAD)

    def backward_block(accumulated, block_args):
        key_grad, value_grad = accumulated
        query_block, grad_block, total_block, index_block, segment_block, parent_block = block_args
        visible = visibility(index_block, segment_block, parent_block, segment_ids)
        scores = block_scores(query_block, visible)
        probs = jnp.where(visible[None], jnp.exp(scores - total_block[..., None]), 0.0)
        probs_low = probs.astype(jnp.bfloat16)
        value_grad = value_grad + jnp.einsum(
            "hqk,qhe->khe", probs_low, grad_block, preferred_element_type=jnp.float32
        )
        grad_probs = jnp.einsum(
            "qhe,khe->hqk", grad_block, values_all, preferred_element_type=jnp.float32
        )
        delta_sum = jnp.sum(probs * grad_probs, axis=-1, keepdims=True)
        grad_scores = (probs * (grad_probs - delta_sum)).astype(jnp.bfloat16)
        grad_query = (
            jnp.einsum("hqk,khe->qhe", grad_scores, keys_all, preferred_element_type=jnp.float32)
            * score_scale
        )
        key_grad = (
            key_grad
            + jnp.einsum(
                "hqk,qhe->khe", grad_scores, query_block, preferred_element_type=jnp.float32
            )
            * score_scale
        )
        return ((key_grad, value_grad), grad_query)

    zero_heads = jnp.zeros((tree_len, local_heads, HEAD), jnp.float32)
    (grad_keys, grad_values), grad_queries = lax.scan(
        backward_block,
        (zero_heads, zero_heads),
        (query_blocks, grad_attended_blocks, log_total, row_index, segment_blocks, parent_blocks),
    )
    grad_queries = grad_queries.reshape(tree_len, local_heads, HEAD)
    grad_projected = jnp.stack(
        [
            rotary(grad_queries, cosine, -sine_part).reshape(tree_len, head_width),
            rotary(grad_keys, cosine, -sine_part).reshape(tree_len, head_width),
            grad_values.reshape(tree_len, head_width),
        ]
    ).astype(jnp.bfloat16)
    grad_head = jnp.einsum(
        "td,stf->sdf", gathered_one, grad_projected, preferred_element_type=jnp.float32
    )
    grad_normed_all = jnp.einsum(
        "stf,sdf->td", grad_projected, head_back, preferred_element_type=jnp.float32
    )
    grad_normed_one = lax.psum_scatter(
        grad_normed_all.astype(jnp.bfloat16), "tensor", scatter_dimension=0, tiled=True
    ).astype(jnp.float32)
    grad_head_own, grad_output_own = (
        lax.psum_scatter(grad_head, "dp", scatter_dimension=1, tiled=True),
        lax.psum_scatter(grad_output_weight, "dp", scatter_dimension=1, tiled=True),
    )
    norm_values, pull_norm = jax.vjp(normed, token_values, attention_gain)
    grad_token_part, grad_attention_gain = pull_norm(grad_normed_one)
    grad_tokens = grad_hidden + grad_token_part
    summed_small = lax.psum(
        (
            grad_attention_gain,
            grad_expert_gain,
            grad_router,
            grad_carry,
            grad_constant_gate,
            grad_constant_vector,
        ),
        ("dp", "tensor"),
    )
    return (
        output,
        grad_tokens,
        grad_carried,
        summed_small[0],
        grad_head_own,
        grad_output_own,
        summed_small[1],
        summed_small[2],
        summed_small[3],
        summed_small[4],
        summed_small[5],
        grad_first_own,
        grad_second_own,
    )


def solution(mesh):
    in_specs = (
        P(("dp", "tensor"), None),
        P(("dp", "tensor"), None),
        P(("dp", "tensor"), None),
        P("dp"),
        P("dp"),
        P("dp", None),
        P(),
        P(None, "dp", "tensor"),
        P("tensor", "dp"),
        P(),
        P(),
        P(),
        P(),
        P(),
        P(None, None, "dp", "tensor"),
        P(None, "tensor", "dp"),
    )
    out_specs = (
        P(("dp", "tensor"), None),
        P(("dp", "tensor"), None),
        P(("dp", "tensor"), None),
        P(),
        P(None, "dp", "tensor"),
        P("tensor", "dp"),
        P(),
        P(),
        P(),
        P(),
        P(),
        P(None, None, "dp", "tensor"),
        P(None, "tensor", "dp"),
    )
    return jax.shard_map(
        per_device, mesh=mesh, in_specs=in_specs, out_specs=out_specs, check_vma=False
    )
```

profile of v0, /device:TPU:0, one launch (start us, length us, event | category | flops | bytes accessed | tf_op | source)
XLA Modules:
  0.0 1865.4 jit_solution(7418865816720089129)
XLA Ops:
  11.3 38.6 %all_gather.32 = bf16[3,768,192]{2,0,1:T(4,128)(2,1)S(1)} all-gather(bf16[3,96,192]{2,0,1:T(4,128)(2,1)S(1)} %copy.105), channel_id=1, replica_groups=mesh['dp'=8,'tensor'=4] {'dp'}, dimensions={1}, use_global_device_ids=true | all-gather | bytes 995328 | tf_op jit(solution)/shard_map/all_gather | solution.py:159
  51.4 31.0 %all_gather.33 = bf16[192,768]{0,1:T(8,128)(2,1)S(1)} all-gather(bf16[192,96]{0,1:T(8,128)(2,1)S(1)} %copy.110), channel_id=1, replica_groups=mesh['dp'=8,'tensor'=4] {'dp'}, dimensions={1}, use_global_device_ids=true | all-gather | bytes 331776 | tf_op jit(solution)/shard_map/all_gather | solution.py:160
  90.2 89.0 %while.27 = (s32[]{:T(128)}, bf16[4,512,3,64]{1,3,2,0:T(8,128)(2,1)S(1)}, f32[4,3,512]{2,1,0:T(4,128)}, s32[4,512]{1,0:T(4,128)S(1)}, s32[2048]{0:T(1024)S(1)}, ...) while((s32[]{:T(128)}, ...), condition=%wide.region_8.9_spmd, body=%wide.region_5.8_spmd.sunk | while | flops 849347072 | bytes 44200072 | solution.py:201
  98.2 6.8 fusion.192
  104.9 6.9 fusion.193
  120.4 6.8 fusion.192
  127.2 6.9 fusion.193
  142.6 6.8 fusion.192
  149.4 6.9 fusion.193
  164.9 6.8 fusion.192
  171.6 6.9 fusion.193
  187.4 55.3 %reduce-scatter.14.cloned.1.call-done = f32[512,768]{1,0:T(8,128)} async-done(((f32[2048,768]{1,0:T(8,128)}), f32[512,768]{1,0:T(8,128)}) %reduce-scatter.14.cloned.1.call-update) | async-done | bytes 1572880 | tf_op jit(solution)/shard_map/reduce_scatter | solution.py:206
  283.9 7.4 reduce-window.19
  298.0 16.1 scatter_custom_fusion
  314.7 22.7 %gather_fusion.2 = bf16[4096,768]{1,0:T(8,128)(2,1)} fusion(bf16[2048,768]{1,0:T(8,128)(2,1)} %all-gather.15.cloned.1.call-done, s32[4096]{0:T(1024)} %get-tuple-element.421), kind=kCustom, calls=%fused_computation.2 | custom fusion | bytes 12599296 | tf_op jit(solution)/shard_map/gather | solution.py:259
  337.4 22.4 %gather_fusion = bf16[4096,768]{1,0:T(8,128)(2,1)} fusion(bf16[2048,768]{1,0:T(8,128)(2,1)} %all-gather.9.cloned.1.call-done, s32[4096]{0:T(1024)} %get-tuple-element.421), kind=kCustom, calls=%fused_computation | custom fusion | bytes 12599296 | tf_op jit(solution)/shard_map/gather | solution.py:232
  359.8 123.2 %all-gather.11.cloned.1.call-done = bf16[8,2,768,512]{3,2,1,0:T(8,128)(2,1)} async-done(((bf16[8,2,96,512]{3,2,1,0:T(8,128)(2,1)}), bf16[8,2,768,512]{3,2,1,0:T(8,128)(2,1)}) %all-gather.11.cloned.1.call-update) | async-done | bytes 12582928 | tf_op jit(solution)/shard_map/all_gather | solution.py:224
  483.0 15.6 convolution_bitcast_fusion.1
  498.6 8.6 multiply_convert_fusion.3
  507.2 75.9 %all-gather.13.cloned.1.call-done = bf16[8,512,768]{1,2,0:T(8,128)(2,1)} async-done(((bf16[8,512,96]{1,2,0:T(8,128)(2,1)}), bf16[8,512,768]{1,2,0:T(8,128)(2,1)}) %all-gather.13.cloned.1.call-update) | async-done | bytes 6291472 | tf_op jit(solution)/shard_map/all_gather | solution.py:225
  583.1 13.7 fusion.39
  597.4 26.8 %scatter_custom_fusion.3 = f32[4096]{0:T(1024)} fusion(s32[4096]{0:T(1024)} %get-tuple-element.420, f32[4096]{0:T(1024)} %bitcast.324, f32[]{:T(128)} %constant.75.clone.1), kind=kCustom, calls=%fused_computation.217 | custom fusion | flops 4096 | bytes 16896 | tf_op jit(solution)/shard_map/scatter-add | solution.py:266
  627.6 22.6 %reduce-scatter.20.cloned.1.call-done = f32[512,2]{1,0:T(8,128)} async-done(((f32[2048,2]{1,0:T(8,128)}), f32[512,2]{1,0:T(8,128)}) %reduce-scatter.20.cloned.1.call-update) | async-done | bytes 4112 | tf_op jit(solution)/shard_map/reduce_scatter | solution.py:288
  653.4 7.0 all_gather.37
  661.0 25.7 %gather_fusion.1 = bf16[4096]{0:T(1024)(128)(2,1)S(1)} fusion(bf16[4096]{0:T(1024)(128)(2,1)S(1)} %reshape.593, s32[4096]{0:T(1024)} %get-tuple-element.419), kind=kCustom, calls=%fused_computation.1 | custom fusion | bytes 32768 | tf_op jit(solution)/shard_map/gather | solution.py:231
  686.7 14.4 fusion.48
  701.1 13.6 fusion.40
  714.8 31.2 %scatter_custom_fusion.2 = f32[2048,768]{1,0:T(8,128)} fusion(s32[4096]{0:T(1024)} %get-tuple-element.422, f32[4096,768]{1,0:T(8,128)} %bitcast.328, f32[]{:T(128)} %constant.75.clone.1), kind=kCustom, calls=%fused_computation.92 | custom fusion | flops 3145728 | bytes 6291968 | tf_op jit(solution)/shard_map/scatter-add | solution.py:285
  746.3 11.7 bitcast_multiply_fusion
  758.0 31.3 %scatter_custom_fusion.1 = f32[2048,768]{1,0:T(8,128)} fusion(s32[4096]{0:T(1024)} %get-tuple-element.422, f32[4096,768]{1,0:T(8,128)} %bitcast_multiply_fusion, f32[]{:T(128)} %constant.75.clone.1), kind=kCustom, calls=%fused_computation.94 | custom fusion | flops 3145728 | bytes 6291968 | tf_op jit(solution)/shard_map/scatter-add | solution.py:245
  810.9 35.4 %reduce-scatter.16.cloned.1.call-done = bf16[512,768]{1,0:T(8,128)(2,1)} async-done(((bf16[2048,768]{1,0:T(8,128)(2,1)}), bf16[512,768]{1,0:T(8,128)(2,1)}) %reduce-scatter.16.cloned.1.call-update) | async-done | bytes 786448 | tf_op jit(solution)/shard_map/reduce_scatter | solution.py:247
  850.2 28.6 %all-gather.17.cloned.1.call-done = bf16[2048,768]{1,0:T(8,128)(2,1)} async-done(((bf16[512,768]{1,0:T(8,128)(2,1)}), bf16[2048,768]{1,0:T(8,128)(2,1)}) %all-gather.17.cloned.1.call-update) | async-done | bytes 3145744 | tf_op jit(solution)/shard_map/all_gather | solution.py:304
  883.5 175.6 %while.28 = (s32[]{:T(128)}, f32[2048,3,64]{0,2,1:T(8,128)}, f32[2048,3,64]{0,2,1:T(8,128)}, f32[4,512,3,64]{1,0,3,2:T(4,128)}, bf16[4,512,3,64]{1,3,2,0:T(8,128...) while((s32[]{:T(128)}, f32[2048,3,64]{0,2,1:T(8,128)}, ...), condition=%wide.region_41.42_spmd.clone, body=%wide.region_39.41_spmd.clone.sunk | while | flops 2053079552 | bytes 192876944 | solution.py:342
  918.7 8.6 dynamic_update_slice.19
  935.3 6.3 multiply_reduce_fusion.7
  962.6 8.6 dynamic_update_slice.19
  979.2 6.3 multiply_reduce_fusion.7
  1006.5 8.6 dynamic_update_slice.19
  1023.1 6.3 multiply_reduce_fusion.7
  1050.4 8.6 dynamic_update_slice.19
  1086.9 16.1 convolution_bitcast_fusion
  1103.0 25.1 %copy.122 = f32[8,2,768,512]{3,0,1,2:T(8,128)} copy(f32[8,2,768,512]{2,3,1,0:T(8,128)} %convolution_bitcast_fusion) | data formatting | bytes 50331648 | tf_op jit(solution)/shard_map/ecd,escf->esdf/transpose | solution.py:279
  1128.8 12.2 fusion.43
  1147.9 51.1 %reduce-scatter.28.cloned.1.call-done = f32[96,576]{1,0:T(8,128)} async-done(((f32[768,576]{1,0:T(8,128)}), f32[96,576]{1,0:T(8,128)}) %reduce-scatter.28.cloned.1.call-update) | async-done | bytes 221200
  1202.7 36.4 %reduce-scatter.22.cloned.1.call-done = bf16[512,768]{1,0:T(8,128)(2,1)} async-done(((bf16[2048,768]{1,0:T(8,128)(2,1)}), bf16[512,768]{1,0:T(8,128)(2,1)}) %reduce-scatter.22.cloned.1.call-update) | async-done | bytes 786448 | tf_op jit(solution)/shard_map/reduce_scatter | solution.py:361
  1241.0 45.7 %all-reduce.6 = (f32[768]{0:T(1024)}, f32[768]{0:T(1024)}, f32[768,12]{0,1:T(8,128)}, f32[12,12]{0,1:T(8,128)S(1)}, f32[768,4]{0,1:T(4,128)}, /*index=5*/f32[2,768]{1,0:T(2,128)}) all-reduce(f32[768]{0:T(1024)S(1)} %get-tuple-element.319, f32[768]{0:T(1024)S(1)} %copy-done.100, ...), channel_id=1, replica_groups=mesh['dp'=8,'tensor'=4] {'dp','tensor'}, use_global_device_ids=true, to_apply=%region_45.46 | all-reduce | flops 15504 | bytes 124032 | tf_op jit(solution)/shard_map/psum | solution.py:371
  1291.0 356.5 %reduce-scatter.24.cloned.1.call-done = f32[8,2,96,512]{3,0,1,2:T(8,128)} async-done(((f32[8,2,768,512]{3,0,1,2:T(8,128)}), f32[8,2,96,512]{3,0,1,2:T(8,128)}) %reduce-scatter.24.cloned.1.call-update) | async-done | bytes 3145744 | tf_op jit(solution)/shard_map/reduce_scatter | solution.py:291
  1652.9 205.5 %reduce-scatter.26.cloned.1.call-done = f32[8,512,96]{1,2,0:T(8,128)} async-done(((f32[8,512,768]{1,2,0:T(8,128)}), f32[8,512,96]{1,2,0:T(8,128)}) %reduce-scatter.26.cloned.1.call-update) | async-done | bytes 1572880 | tf_op jit(solution)/shard_map/reduce_scatter | solution.py:292
  (475 shorter events, 313.3 us)
Async XLA Ops:
  7.2 237.9 %copy-start = (f32[768,12]{0,1:T(8,128)S(1)}, f32[768,12]{0,1:T(8,128)}, u32[]{:S(2)}) copy-start(f32[768,12]{0,1:T(8,128)} %param.30) | copy-start | bytes 110596
  7.2 77.0 %all-gather.7.cloned.1.call-start = ((), (), s32[]{:S(2)}) async-start(), calls=%async_computation.9 | async-start | bytes 3932160 | tf_op jit(solution)/shard_map/all_gather | solution.py:164
  11.0 40.1 %copy-start.48 = (f32[192,96]{1,0:T(8,128)S(1)}, f32[192,96]{1,0:T(8,128)}, u32[]{:S(2)}) copy-start(f32[192,96]{1,0:T(8,128)} %param.28) | copy-start | bytes 221188
  11.0 231.8 %reduce-scatter.14.cloned.1.call-start = ((), (), s32[]{:S(2)}) async-start(), calls=%async_computation.10 | async-start | bytes 7864320 | tf_op jit(solution)/shard_map/reduce_scatter | solution.py:206
  50.8 37.4 %copy-start.28 = (bf16[3,768,192]{1,2,0:T(8,128)(2,1)}, bf16[3,768,192]{1,2,0:T(8,128)(2,1)S(1)}, u32[]{:S(2)}) copy-start(bf16[3,768,192]{1,2,0:T(8,128)(2,1)S(1)} %copy.106) | copy-start | bytes 2654212
  82.4 97.6 %copy-start.22 = (bf16[192,768]{0,1:T(8,128)(2,1)}, bf16[192,768]{0,1:T(8,128)(2,1)S(1)}, u32[]{:S(2)}) copy-start(bf16[192,768]{0,1:T(8,128)(2,1)S(1)} %all_gather.33) | copy-start | bytes 884740
  184.6 58.2 %copy-start.11 = (bf16[512,768]{1,0:T(8,128)(2,1)S(1)}, bf16[512,768]{1,0:T(8,128)(2,1)}, u32[]{:S(2)}) copy-start(bf16[512,768]{1,0:T(8,128)(2,1)} %param.20) | copy-start | bytes 2359300
  184.7 60.4 %copy-start.37 = (f32[768]{0:T(1024)S(1)}, f32[768]{0:T(1024)}, u32[]{:S(2)}) copy-start(f32[768]{0:T(1024)} %param.29) | copy-start | bytes 9220
  184.7 130.0 %all-gather.15.cloned.1.call-start = ((), (), s32[]{:S(2)}) async-start(), calls=%async_computation.15 | async-start | bytes 3932160 | tf_op jit(solution)/shard_map/all_gather | solution.py:258
  185.4 152.0 %all-gather.9.cloned.1.call-start = ((), (), s32[]{:S(2)}) async-start(), calls=%async_computation.11 | async-start | bytes 3932160 | tf_op jit(solution)/shard_map/all_gather | solution.py:220
  186.0 60.6 %copy-start.43 = (f32[512,12]{0,1:T(8,128)S(1)}, f32[512,12]{0,1:T(8,128)}, u32[]{:S(2)}) copy-start(f32[512,12]{0,1:T(8,128)} %param.21) | copy-start | bytes 73732
  186.7 73.6 %copy-start.61 = (f32[768]{0:T(1024)}, f32[768]{0:T(1024)S(1)}, u32[]{:S(2)}) copy-start(f32[768]{0:T(1024)S(1)} %get-tuple-element.328) | copy-start | bytes 9220
  244.5 601.8 %copy-start.3 = (f32[512,768]{1,0:T(8,128)}, f32[512,768]{1,0:T(8,128)S(1)}, u32[]{:S(2)}) copy-start(f32[512,768]{1,0:T(8,128)S(1)} %get-tuple-element.391) | copy-start | bytes 4718596
  244.5 601.8 %copy-start.40 = (f32[512]{0:T(512)}, f32[512]{0:T(512)S(1)}, u32[]{:S(2)}) copy-start(f32[512]{0:T(512)S(1)} %fusion.109) | copy-start | bytes 6148
  255.8 394.4 %copy-start.57 = (f32[512]{0:T(512)}, f32[512]{0:T(512)S(1)}, u32[]{:S(2)}) copy-start(f32[512]{0:T(512)S(1)} %reduce_max.27) | copy-start | bytes 6148
  264.7 218.3 %all-gather.11.cloned.1.call-start = ((), (), s32[]{:S(2)}) async-start(), calls=%async_computation.12 | async-start | bytes 14155776 | tf_op jit(solution)/shard_map/all_gather | solution.py:224
  268.0 315.1 %all-gather.13.cloned.1.call-start = ((), (), s32[]{:S(2)}) async-start(), calls=%async_computation.13 | async-start | bytes 7077888 | tf_op jit(solution)/shard_map/all_gather | solution.py:225
  270.5 379.7 %reduce-scatter.20.cloned.1.call-start = ((), (), s32[]{:S(2)}) async-start(), calls=%async_computation.17 | async-start | bytes 1310720 | tf_op jit(solution)/shard_map/reduce_scatter | solution.py:288
  277.9 18.1 copy-start.54
  583.1 43.9 %copy-start.77 = (f32[512]{0:T(512)S(1)}, f32[512]{0:T(512)}, u32[]{:S(2)}) copy-start(f32[512]{0:T(512)} %copy-done.76) | copy-start | bytes 6148
  626.9 178.1 %reduce-scatter.18.cloned.1.call-start = ((), (), s32[]{:S(2)}) async-start(), calls=%async_computation.16 | async-start | bytes 7864320 | tf_op jit(solution)/shard_map/reduce_scatter | solution.py:287
  686.7 14.4 copy-start.55
  746.0 100.2 %reduce-scatter.16.cloned.1.call-start = ((), (), s32[]{:S(2)}) async-start(), calls=%async_computation.14 | async-start | bytes 3932160 | tf_op jit(solution)/shard_map/reduce_scatter | solution.py:247
  794.2 84.6 %all-gather.17.cloned.1.call-start = ((), (), s32[]{:S(2)}) async-start(), calls=%async_computation.18 | async-start | bytes 3932160 | tf_op jit(solution)/shard_map/all_gather | solution.py:304
  805.0 41.2 %copy-start.62 = (f32[768]{0:T(1024)S(1)}, f32[768]{0:T(1024)}, u32[]{:S(2)}) copy-start(f32[768]{0:T(1024)} %copy-done.61) | copy-start | bytes 9220
  805.1 41.2 %copy-start.63 = (f32[768]{0:T(1024)S(1)}, f32[768]{0:T(1024)}, u32[]{:S(2)}) copy-start(f32[768]{0:T(1024)} %get-tuple-element.329) | copy-start | bytes 9220
  805.1 41.2 %copy-start.84 = (f32[512,1,1]{0,2,1:T(1,128)S(1)}, f32[512,1,1]{0,2,1:T(1,128)}, u32[]{:S(2)}) copy-start(f32[512,1,1]{0,2,1:T(1,128)} %copy-done.83) | copy-start | bytes 6148
  805.1 41.2 %copy-start.86 = (f32[512,1,1]{0,2,1:T(1,128)S(1)}, f32[512,1,1]{0,2,1:T(1,128)}, u32[]{:S(2)}) copy-start(f32[512,1,1]{0,2,1:T(1,128)} %copy-done.85) | copy-start | bytes 6148
  810.9 39.2 %copy-start.81 = (f32[512]{0:T(512)}, f32[512]{0:T(512)S(1)}, u32[]{:S(2)}) copy-start(f32[512]{0:T(512)S(1)} %multiply_multiply_fusion.2) | copy-start | bytes 6148
  846.3 32.5 %copy-start.23 = (bf16[192,768]{0,1:T(8,128)(2,1)S(1)}, bf16[192,768]{0,1:T(8,128)(2,1)}, u32[]{:S(2)}) copy-start(bf16[192,768]{0,1:T(8,128)(2,1)} %copy-done.22) | copy-start | bytes 884740
  850.1 296.1 %reduce-scatter.30.cloned.1.call-start = ((), (), s32[]{:S(2)}) async-start(), calls=%async_computation.23 | async-start | bytes 884736
  850.2 33.4 %copy-start.19 = (s32[2048]{0:T(1024)S(1)}, s32[2048]{0:T(1024)}, u32[]{:S(2)}) copy-start(s32[2048]{0:T(1024)} %param.23) | copy-start | bytes 24580
  904.6 11.6 slice-start
  948.1 12.1 slice-start
  991.9 12.1 slice-start
  1035.8 12.1 slice-start
  1066.7 132.3 %reduce-scatter.28.cloned.1.call-start = ((), (), s32[]{:S(2)}) async-start(), calls=%async_computation.22 | async-start | bytes 2211840
  1080.5 158.5 %reduce-scatter.22.cloned.1.call-start = ((), (), s32[]{:S(2)}) async-start(), calls=%async_computation.19 | async-start | bytes 3932160 | tf_op jit(solution)/shard_map/reduce_scatter | solution.py:361
  1086.8 560.7 %reduce-scatter.24.cloned.1.call-start = ((), (), s32[]{:S(2)}) async-start(), calls=%async_computation.20 | async-start | bytes 28311552 | tf_op jit(solution)/shard_map/reduce_scatter | solution.py:291
  1128.1 730.3 %reduce-scatter.26.cloned.1.call-start = ((), (), s32[]{:S(2)}) async-start(), calls=%async_computation.21 | async-start | bytes 14155776 | tf_op jit(solution)/shard_map/reduce_scatter | solution.py:292
  1141.0 98.0 %copy-start.12 = (bf16[512,768]{1,0:T(8,128)(2,1)S(1)}, bf16[512,768]{1,0:T(8,128)(2,1)}, u32[]{:S(2)}) copy-start(bf16[512,768]{1,0:T(8,128)(2,1)} %param.20) | copy-start | bytes 2359300
  1141.1 98.0 %copy-start.60 = (f32[768]{0:T(1024)S(1)}, f32[768]{0:T(1024)}, u32[]{:S(2)}) copy-start(f32[768]{0:T(1024)} %param.26) | copy-start | bytes 9220
  1141.1 98.0 %copy-start.75 = (f32[512]{0:T(512)S(1)}, f32[512]{0:T(512)}, u32[]{:S(2)}) copy-start(f32[512]{0:T(512)} %copy-done.74) | copy-start | bytes 6148
  1143.5 97.5 %copy-start.100 = (f32[768]{0:T(1024)S(1)}, f32[768]{0:T(1024)}, u32[]{:S(2)}) copy-start(f32[768]{0:T(1024)} %get-tuple-element.312) | copy-start | bytes 9220
  1143.5 143.8 %copy-start.97 = (f32[512]{0:T(512)S(1)}, f32[512]{0:T(512)}, u32[]{:S(2)}) copy-start(f32[512]{0:T(512)} %copy-done.96) | copy-start | bytes 6148
  1143.5 143.8 %copy-start.14 = (bf16[512,768]{1,0:T(8,128)(2,1)S(1)}, bf16[512,768]{1,0:T(8,128)(2,1)}, u32[]{:S(2)}) copy-start(bf16[512,768]{1,0:T(8,128)(2,1)} %param.22) | copy-start | bytes 2359300
  1143.5 143.8 %copy-start.82 = (f32[512]{0:T(512)S(1)}, f32[512]{0:T(512)}, u32[]{:S(2)}) copy-start(f32[512]{0:T(512)} %copy-done.81) | copy-start | bytes 6148
  1287.4 571.0 %copy-start.1 = (f32[768,12]{0,1:T(8,128)S(1)}, f32[768,12]{0,1:T(8,128)}, u32[]{:S(2)}) copy-start(f32[768,12]{0,1:T(8,128)} %param.30) | copy-start | bytes 110596
  (91 other events, 334.9 us)
Sparse Core Ops, SparseCore 0:
  11.1 31.2 all-gather.6
  184.8 57.9 reduce-scatter.13
  244.4 28.5 all-gather.14
  275.1 28.5 all-gather.8
  306.5 176.4 all-gather.10
  485.8 97.1 all-gather.12
  627.1 23.0 reduce-scatter.19
  746.1 58.8 reduce-scatter.17
  808.3 37.9 reduce-scatter.15
  850.2 28.5 all-gather.16
  1066.8 62.5 reduce-scatter.29
  1133.1 65.8 reduce-scatter.27
  1202.1 36.8 reduce-scatter.21
  1243.3 404.2 reduce-scatter.23
  1652.0 206.3 reduce-scatter.25
where the time goes:
time: 1880 us; the launch traced here: 1870 us
  waiting for transfers between devices  995 us (53%)
  matrix products  279 us (15%)
  other arithmetic  234 us (12%)
  local copies, waits for them, and re-layouts  218 us (12%)
  blocking collectives  122 us (6%)
    reduce_scatter x1, waiting for transfers between devices, per_device(): lax.psum_scatter(grad_first, 'dp', scatter_dimension=2, tiled=True)  357 us
    reduce_scatter x1, waiting for transfers between devices, per_device(): lax.psum_scatter(grad_second, 'dp', scatter_dimension=2, tiled=True)  206 us
    all_gather x1, waiting for transfers between devices, per_device(): lax.all_gather(first_low, 'dp', axis=2, tiled=True)  123 us
    all_gather x1, waiting for transfers between devices, per_device(): lax.all_gather(second_low, 'dp', axis=2, tiled=True)  75.9 us
    reduce_scatter x1, waiting for transfers between devices, per_device(): lax.psum_scatter(attention_part, 'tensor', scatter_dimension=0, tiled=True)  55.3 us
    unnamed x17, waiting for transfers between devices  52.1 us
    dot_general x8, matrix products, block_scores(): jnp.einsum('qhe,khe->hqk', query_block, keys_all, preferred_element_type=...  49.2 us
    psum x1, blocking collectives, per_device(): lax.psum((grad_attention_gain, grad_expert_gain, grad_router, grad_carry,...  45.7 us
  transfers between devices with their start and end apart: 15, of which 11 were waited for; matrix products, arithmetic and copies ran while one was open for 16% of the time, Pallas kernels for 0%

commit v1 on v0

v1 whole, which is shorter than its diff:
```python
import functools

import jax
import jax.numpy as jnp
from jax import lax
from jax.experimental import pallas as pl
from jax.experimental.pallas import tpu as pltpu
from jax.sharding import PartitionSpec as P

HEAD = 64
NF = 8
NSEG = 13
NE = 12
PAD = 256
BLOCK = 256
TILE = 256
GROUPS = 4

epsilon = 1e-06
HIGHEST = lax.Precision.HIGHEST
F32 = jnp.float32
BF16 = jnp.bfloat16


def dot_nn(a, b):
    return lax.dot_general(a, b, (((1,), (0,)), ((), ())), preferred_element_type=F32)


def dot_nt(a, b):
    return lax.dot_general(a, b, (((1,), (1,)), ((), ())), preferred_element_type=F32)


def dot_tn(a, b):
    return lax.dot_general(a, b, (((0,), (0,)), ((), ())), preferred_element_type=F32)


def normed(values, gain_vector):
    return (
        values
        * lax.rsqrt(jnp.mean(values * values, axis=-1, keepdims=True) + epsilon)
        * gain_vector
    )


def tree_positions(segment, parent):
    token_count = segment.shape[0]
    labels = jnp.arange(NSEG, dtype=jnp.int32)
    own_hot = (segment[:, None] == labels[None, :]).astype(jnp.int32)
    parent_hot = (parent[:, None] == labels[None, :]).astype(jnp.int32)
    lengths = jnp.sum(own_hot, axis=0)
    starts = jnp.cumsum(lengths) - lengths
    own_start = jnp.sum(own_hot * starts[None, :], axis=1)
    parent_length = jnp.sum(parent_hot * lengths[None, :], axis=1)
    position_index = jnp.arange(token_count, dtype=jnp.int32)
    return (
        position_index
        - own_start
        + jnp.where(segment > 0, lengths[0], 0)
        + jnp.where(parent > 0, parent_length, 0)
    )


def rotary_tables(segment, parent):
    angle_rate = 10000.0 ** (-2.0 * jnp.arange(HEAD // 2, dtype=F32) / HEAD)
    angles = tree_positions(segment, parent).astype(F32)[:, None] * angle_rate[None, :]
    cosine, sine = jnp.cos(angles), jnp.sin(angles)
    copies = PAD // HEAD
    cos_table = jnp.tile(jnp.concatenate([cosine, cosine], axis=1), (1, copies))
    sin_table = jnp.tile(jnp.concatenate([-sine, sine], axis=1), (1, copies))
    return cos_table, sin_table


def router_local(
    hidden, gain_vector, carried, router_weight, carry_weight, constant_gate, constant_vector, routes
):
    normed_two = normed(hidden, gain_vector)
    logits = jnp.dot(normed_two, router_weight, precision=HIGHEST) + jnp.dot(
        carried, carry_weight, precision=HIGHEST
    )
    picked = (routes[:, :, None] == jnp.arange(NE, dtype=jnp.int32)[None, None, :]).astype(F32)
    chosen = jnp.sum(picked * logits[:, None, :], axis=-1)
    gate_values = jax.nn.softmax(chosen, axis=-1)
    by_expert = jnp.sum(picked * gate_values[:, :, None], axis=1)
    mixture = jax.nn.softmax(
        jnp.dot(normed_two, constant_gate, precision=HIGHEST).reshape(-1, 2, 2), axis=-1
    )
    copy_weight = by_expert[:, NF + 1]
    first_weight = by_expert[:, NF + 2]
    second_weight = by_expert[:, NF + 3]
    local_sum = copy_weight[:, None] * normed_two
    local_sum = local_sum + first_weight[:, None] * (
        mixture[:, 0, 0:1] * normed_two + mixture[:, 0, 1:2] * constant_vector[0][None, :]
    )
    local_sum = local_sum + second_weight[:, None] * (
        mixture[:, 1, 0:1] * normed_two + mixture[:, 1, 1:2] * constant_vector[1][None, :]
    )
    return (normed_two, by_expert[:, :NF], local_sum)


def swap(values, axis, bits):
    size = lax.axis_size(axis)
    return lax.ppermute(values, axis, [(i, i ^ bits) for i in range(size)])


def gather_tensor(own):
    index = lax.axis_index("tensor")
    far = swap(own, "tensor", 2)
    near = swap(own, "tensor", 1)
    far_near = swap(far, "tensor", 1)
    core, chip = index % 2 == 0, index // 2 == 0
    here = [jnp.where(core, own, near), jnp.where(core, near, own)]
    there = [jnp.where(core, far, far_near), jnp.where(core, far_near, far)]
    order = [jnp.where(chip, h, t) for h, t in zip(here, there)]
    order += [jnp.where(chip, t, h) for h, t in zip(here, there)]
    return jnp.concatenate(order, axis=0)


def scatter_tensor(parts, rows):
    index = lax.axis_index("tensor")

    def take(which):
        return lax.dynamic_slice_in_dim(parts, which * rows, rows, 0).astype(F32)

    near = swap(
        jnp.concatenate([take(index ^ 1), take(index ^ 3)], axis=0).astype(BF16), "tensor", 1
    ).astype(F32)
    mine = take(index) + near[:rows]
    other = take(index ^ 2) + near[rows:]
    return mine + swap(other.astype(BF16), "tensor", 2).astype(F32)


def pieces_of(own, axis):
    if lax.axis_size("dp") != 8:
        return [lax.all_gather(own, "dp", axis=axis, tiled=True)]
    column = [own, swap(own, "dp", 2), swap(own, "dp", 4), swap(own, "dp", 6)]
    pieces = []
    for shard in column:
        pieces += [shard, swap(shard, "dp", 1)]
    return pieces


def sum_pieces(mine, theirs):
    paired = mine.astype(F32) + swap(theirs, "dp", 1).astype(F32)
    total = paired[0]
    for j in range(1, 4):
        total = total + swap(paired[j].astype(BF16), "dp", 2 * j).astype(F32)
    return total


def sum_all(values):
    if lax.axis_size("dp") != 8:
        return lax.psum(values, ("dp", "tensor"))
    for axis, bits in (("tensor", 1), ("tensor", 2), ("dp", 1), ("dp", 2), ("dp", 4)):
        values = values + swap(values, axis, bits)
    return values


def swap_halves(values):
    lane = lax.broadcasted_iota(jnp.int32, values.shape, 1)
    half = HEAD // 2
    return jnp.where(
        lane % HEAD < half, pltpu.roll(values, PAD - half, 1), pltpu.roll(values, half, 1)
    )


def project_kernel(n_ref, w_ref, c_ref, s_ref, q_ref, k_ref, v_ref, kt_ref, vt_ref):
    rows = n_ref[...]
    cosine, sine = c_ref[...], s_ref[...]
    part = dot_nn(rows, w_ref[:, :PAD])
    q_ref[...] = ((part * cosine + swap_halves(part) * sine) * HEAD**-0.5).astype(BF16)
    part = dot_nn(rows, w_ref[:, PAD : 2 * PAD])
    keys = part * cosine + swap_halves(part) * sine
    k_ref[...] = keys.astype(BF16)
    kt_ref[...] = keys.T.astype(BF16)
    values = dot_nn(rows, w_ref[:, 2 * PAD : 3 * PAD])
    v_ref[...] = values.astype(BF16)
    vt_ref[...] = values.T.astype(BF16)


def project(gathered, weights, cos_table, sin_table):
    rows, width = gathered.shape
    grid = (rows // BLOCK,)
    row_spec = pl.BlockSpec((BLOCK, PAD), lambda i: (i, 0))
    column_spec = pl.BlockSpec((PAD, BLOCK), lambda i: (0, i))
    wide = jax.ShapeDtypeStruct((rows, PAD), BF16)
    tall = jax.ShapeDtypeStruct((PAD, rows), BF16)
    return pl.pallas_call(
        project_kernel,
        grid=grid,
        in_specs=[
            pl.BlockSpec((BLOCK, width), lambda i: (i, 0)),
            pl.BlockSpec(weights.shape, lambda i: (0, 0)),
            row_spec,
            row_spec,
        ],
        out_specs=[row_spec, row_spec, row_spec, column_spec, column_spec],
        out_shape=[wide, wide, wide, tall, tall],
        cost_estimate=pl.CostEstimate(
            flops=2 * rows * width * 3 * PAD, bytes_accessed=8 * rows * width, transcendentals=0
        ),
    )(gathered, weights, cos_table, sin_table)


def head_mask(values, head):
    lane = lax.broadcasted_iota(jnp.int32, values.shape, 1)
    return jnp.where(lane // HEAD == head, values, jnp.zeros_like(values))


def seen(i, j, seg_row, par_row, seg_col):
    key_at = j * BLOCK + lax.broadcasted_iota(jnp.int32, (BLOCK, 1), 0)
    query_at = i * BLOCK + lax.broadcasted_iota(jnp.int32, (1, BLOCK), 1)
    related = (seg_col == seg_row) | (seg_col == par_row) | (seg_col == 0)
    return related & (key_at <= query_at)


def attend_kernel(heads, q_ref, k_ref, vt_ref, rowinfo_ref, colinfo_ref, o_ref, total_ref):
    i = pl.program_id(0)
    queries = q_ref[...]
    by_head = [head_mask(queries, h) for h in range(heads)]
    seg_row, par_row = rowinfo_ref[0:1, :], rowinfo_ref[1:2, :]

    def step(j, carry):
        at = pl.ds(pl.multiple_of(j * BLOCK, BLOCK), BLOCK)
        keys = k_ref[at, :]
        visible = seen(i, j, seg_row, par_row, colinfo_ref[at, 0:1])
        out = []
        for h in range(heads):
            top, total, mixed = carry[h]
            scores = jnp.where(visible, dot_nt(keys, by_head[h]), -1e30)
            new_top = jnp.maximum(top, jnp.max(scores, axis=0, keepdims=True))
            shrink = jnp.exp(top - new_top)
            probs = jnp.exp(scores - new_top)
            total = total * shrink + jnp.sum(probs, axis=0, keepdims=True)
            mixed = mixed * shrink + dot_nn(
                vt_ref[h * HEAD : (h + 1) * HEAD, at], probs.astype(BF16)
            )
            out.append((new_top, total, mixed))
        return tuple(out)

    start = tuple(
        (
            jnp.full((1, BLOCK), -1e30, F32),
            jnp.zeros((1, BLOCK), F32),
            jnp.zeros((HEAD, BLOCK), F32),
        )
        for _ in range(heads)
    )
    done = lax.fori_loop(0, i + 1, step, start)
    mixed = [m / t for _, t, m in done] + [jnp.zeros((PAD - heads * HEAD, BLOCK), F32)]
    o_ref[...] = jnp.concatenate(mixed, axis=0).T.astype(BF16)
    total_ref[...] = jnp.concatenate(
        [m + jnp.log(t) for m, t, _ in done] + [jnp.zeros((8 - heads, BLOCK), F32)], axis=0
    )


def attend(heads, queries, keys, values_t, rowinfo, colinfo):
    rows = queries.shape[0]
    whole = lambda a: pl.BlockSpec(a.shape, lambda i: (0,) * a.ndim)
    return pl.pallas_call(
        functools.partial(attend_kernel, heads),
        grid=(rows // BLOCK,),
        in_specs=[
            pl.BlockSpec((BLOCK, PAD), lambda i: (i, 0)),
            whole(keys),
            whole(values_t),
            pl.BlockSpec((8, BLOCK), lambda i: (0, i)),
            whole(colinfo),
        ],
        out_specs=[
            pl.BlockSpec((BLOCK, PAD), lambda i: (i, 0)),
            pl.BlockSpec((8, BLOCK), lambda i: (0, i)),
        ],
        out_shape=[
            jax.ShapeDtypeStruct((rows, PAD), BF16),
            jax.ShapeDtypeStruct((8, rows), F32),
        ],
        compiler_params=pltpu.CompilerParams(vmem_limit_bytes=32 << 20),
        cost_estimate=pl.CostEstimate(
            flops=heads * rows * rows * 512, bytes_accessed=8 * rows * PAD, transcendentals=0
        ),
    )(queries, keys, values_t, rowinfo, colinfo)


def attend_back_kernel(
    heads,
    q_ref,
    g_ref,
    o_ref,
    k_ref,
    v_ref,
    kt_ref,
    rowinfo_ref,
    colinfo_ref,
    total_ref,
    c_ref,
    s_ref,
    gq_ref,
    gk_ref,
    gv_ref,
    key_sum,
    value_sum,
    query_sum,
):
    i = pl.program_id(0)
    here = pl.ds(pl.multiple_of(i * BLOCK, BLOCK), BLOCK)

    @pl.when(i == 0)
    def _():
        key_sum[...] = jnp.zeros_like(key_sum)
        value_sum[...] = jnp.zeros_like(value_sum)

    query_sum[...] = jnp.zeros_like(query_sum)
    queries, grads = q_ref[...], g_ref[...]
    q_heads = [head_mask(queries, h) for h in range(heads)]
    g_heads = [head_mask(grads, h) for h in range(heads)]
    seg_row, par_row = rowinfo_ref[0:1, :], rowinfo_ref[1:2, :]
    product = grads.astype(F32) * o_ref[...].astype(F32)
    lane = lax.broadcasted_iota(jnp.int32, (8, PAD), 1)
    which = lax.broadcasted_iota(jnp.int32, (8, PAD), 0)
    delta = lax.dot_general(
        (lane // HEAD == which).astype(F32),
        product,
        (((1,), (1,)), ((), ())),
        precision=HIGHEST,
        preferred_element_type=F32,
    )
    totals = total_ref[...]

    def step(j, carry):
        at = pl.ds(pl.multiple_of(j * BLOCK, BLOCK), BLOCK)
        keys, values = k_ref[at, :], v_ref[at, :]
        visible = seen(i, j, seg_row, par_row, colinfo_ref[at, 0:1])
        key_part, value_part = key_sum[at, :], value_sum[at, :]
        for h in range(heads):
            scores = jnp.where(visible, dot_nt(keys, q_heads[h]), -1e30)
            probs = jnp.exp(scores - totals[h : h + 1, :])
            value_part = value_part + dot_nn(probs.astype(BF16), g_heads[h])
            grad_probs = dot_nt(values, g_heads[h])
            grad_scores = (probs * (grad_probs - delta[h : h + 1, :])).astype(BF16)
            key_part = key_part + dot_nn(grad_scores, q_heads[h])
            lanes = slice(h * HEAD, (h + 1) * HEAD)
            query_sum[lanes, :] += dot_nn(kt_ref[lanes, at], grad_scores)
        key_sum[at, :] = key_part
        value_sum[at, :] = value_part
        return carry

    lax.fori_loop(0, i + 1, step, 0)
    grad_q = query_sum[...].T * HEAD**-0.5
    cosine, sine = c_ref[here, :], s_ref[here, :]
    gq_ref[...] = (grad_q * cosine - swap_halves(grad_q) * sine).astype(BF16)

    @pl.when(i == pl.num_programs(0) - 1)
    def _():
        def finish(j, carry):
            at = pl.ds(pl.multiple_of(j * BLOCK, BLOCK), BLOCK)
            grad_k = key_sum[at, :]
            gk_ref[at, :] = (grad_k * c_ref[at, :] - swap_halves(grad_k) * s_ref[at, :]).astype(BF16)
            gv_ref[at, :] = value_sum[at, :].astype(BF16)
            return carry

        lax.fori_loop(0, pl.num_programs(0), finish, 0)


def attend_back(heads, queries, grads, out, keys, values, keys_t, rowinfo, colinfo, totals, cos_table, sin_table):
    rows = queries.shape[0]
    whole = lambda a: pl.BlockSpec(a.shape, lambda i: (0,) * a.ndim)
    row_spec = pl.BlockSpec((BLOCK, PAD), lambda i: (i, 0))
    wide = jax.ShapeDtypeStruct((rows, PAD), BF16)
    return pl.pallas_call(
        functools.partial(attend_back_kernel, heads),
        grid=(rows // BLOCK,),
        in_specs=[
            row_spec,
            row_spec,
            row_spec,
            whole(keys),
            whole(values),
            whole(keys_t),
            pl.BlockSpec((8, BLOCK), lambda i: (0, i)),
            whole(colinfo),
            pl.BlockSpec((8, BLOCK), lambda i: (0, i)),
            whole(cos_table),
            whole(sin_table),
        ],
        out_specs=[
            row_spec,
            pl.BlockSpec((rows, PAD), lambda i: (0, 0)),
            pl.BlockSpec((rows, PAD), lambda i: (0, 0)),
        ],
        out_shape=[wide, wide, wide],
        scratch_shapes=[
            pltpu.VMEM((rows, PAD), F32),
            pltpu.VMEM((rows, PAD), F32),
            pltpu.VMEM((PAD, BLOCK), F32),
        ],
        compiler_params=pltpu.CompilerParams(vmem_limit_bytes=40 << 20),
        cost_estimate=pl.CostEstimate(
            flops=heads * rows * rows * 1280, bytes_accessed=16 * rows * PAD, transcendentals=0
        ),
    )(queries, grads, out, keys, values, keys_t, rowinfo, colinfo, totals, cos_table, sin_table)


def experts_kernel(
    first, n_in, n_out, counts_ref, place_ref, rows_ref, grads_ref, slot_row_ref, gate_row_ref,
    slot_col_ref, gate_col_ref, *refs
):
    in_refs, refs = refs[:n_in], refs[n_in:]
    sum_ref, grad_in_ref, gate_grad_ref = refs[:3]
    out_refs, refs = refs[3 : 3 + n_out], refs[3 + n_out :]
    weight, grad_weight, sum_acc, grad_in_acc = refs
    step = pl.program_id(0)
    expert = first + step
    tokens, width = rows_ref.shape
    hidden = weight.shape[2]
    span = 512

    @pl.when(step == 0)
    def _():
        sum_acc[...] = jnp.zeros_like(sum_acc)
        grad_in_acc[...] = jnp.zeros_like(grad_in_acc)
        gate_grad_ref[...] = jnp.zeros_like(gate_grad_ref)

    grad_weight[...] = jnp.zeros_like(grad_weight)
    if n_in == 1:
        weight[...] = in_refs[0][0]
    else:
        share = width // n_in
        for k in range(n_in):
            at = pl.ds(pl.multiple_of(place_ref[k] * share, share), share)
            weight[:, at, :] = in_refs[k][0]

    lane = lax.broadcasted_iota(jnp.int32, slot_col_ref.shape, 1)
    slot_col = jnp.sum(jnp.where(lane == expert, slot_col_ref[...], 0), axis=1, keepdims=True)
    gate_col = jnp.sum(jnp.where(lane == expert, gate_col_ref[...], 0.0), axis=1, keepdims=True)
    slot_row, gate_row = slot_row_ref[0], gate_row_ref[0]

    def tile(c, carry):
        down = c * TILE + lax.broadcasted_iota(jnp.int32, (TILE, 1), 0)
        across = c * TILE + lax.broadcasted_iota(jnp.int32, (1, TILE), 1)
        picked = slot_row == down
        inputs = dot_nn(jnp.where(picked, 1.0, 0.0).astype(BF16), rows_ref[...]).astype(BF16)
        grad_out = dot_nn(jnp.where(picked, gate_row, 0.0).astype(BF16), grads_ref[...]).astype(BF16)
        gate_part = dot_nn(inputs, weight[0])
        up_part = dot_nn(inputs, weight[1])
        sigmoid = 1.0 / (1.0 + jnp.exp(-gate_part))
        swish = gate_part * sigmoid
        act = (swish * up_part).astype(BF16)
        expert_out = dot_nt(act, weight[2]).astype(BF16)
        grad_act = dot_nn(grad_out, weight[2])
        grad_gate = (grad_act * up_part * sigmoid * (1.0 + gate_part * (1.0 - sigmoid))).astype(BF16)
        grad_up = (grad_act * swish).astype(BF16)
        grad_weight[0] += dot_tn(inputs, grad_gate)
        grad_weight[1] += dot_tn(inputs, grad_up)
        grad_weight[2] += dot_tn(grad_out, act)
        grad_in = (dot_nt(grad_gate, weight[0]) + dot_nt(grad_up, weight[1])).astype(BF16)
        for b in range(tokens // span):
            at = pl.ds(b * span, span)
            back = jnp.where(slot_col[b * span : (b + 1) * span] == across, 1.0, 0.0).astype(BF16)
            part = dot_nn(back, expert_out)
            sum_acc[at, :] += gate_col[b * span : (b + 1) * span] * part
            along = jnp.sum(part * grads_ref[at, :].astype(F32), axis=1, keepdims=True)
            lanes = lax.broadcasted_iota(jnp.int32, (span, gate_grad_ref.shape[1]), 1)
            gate_grad_ref[at, :] += jnp.where(lanes == expert, along, 0.0)
            grad_in_acc[at, :] += dot_nn(back, grad_in)
        return carry

    lax.fori_loop(0, (counts_ref[expert] + TILE - 1) // TILE, tile, 0)

    if n_out == 1:
        out_refs[0][0] = grad_weight[...].astype(BF16)
    else:
        for j in range(n_in // 2):
            for which in range(2):
                at = pl.ds(pl.multiple_of(place_ref[2 * j + which] * share, share), share)
                out_refs[which][j, 0] = grad_weight[:, at, :].astype(BF16)

    @pl.when(step == pl.num_programs(0) - 1)
    def _():
        sum_ref[...] = sum_acc[...].astype(BF16)
        grad_in_ref[...] = grad_in_acc[...].astype(BF16)


def experts(first, pieces, counts, place, rows, grads, slot_rows, gate_rows, slot_cols, gate_cols):
    tokens, width = rows.shape
    group, kinds, share, hidden = pieces[0].shape
    n_in = len(pieces)
    whole = lambda a: pl.BlockSpec(a.shape, lambda e, *_: (0,) * a.ndim, pipeline_mode=pl.Buffered(1))
    by_expert = pl.BlockSpec((1, 1, tokens), lambda e, *_: (first + e, 0, 0))
    piece_spec = pl.BlockSpec((1, kinds, share, hidden), lambda e, *_: (e, 0, 0, 0))
    token_spec = lambda w: pl.BlockSpec((tokens, w), lambda e, *_: (0, 0), pipeline_mode=pl.Buffered(1))
    if n_in == 1:
        grad_specs = [piece_spec]
        grad_shapes = [jax.ShapeDtypeStruct(pieces[0].shape, BF16)]
    else:
        half = n_in // 2
        grad_specs = [pl.BlockSpec((half, 1, kinds, share, hidden), lambda e, *_: (0, e, 0, 0, 0))] * 2
        grad_shapes = [jax.ShapeDtypeStruct((half, group, kinds, share, hidden), BF16)] * 2
    slots = tokens // 4
    return pl.pallas_call(
        functools.partial(experts_kernel, first, n_in, len(grad_specs)),
        grid_spec=pltpu.PrefetchScalarGridSpec(
            num_scalar_prefetch=2,
            grid=(group,),
            in_specs=[whole(rows), whole(grads), by_expert, by_expert, whole(slot_cols), whole(gate_cols)]
            + [piece_spec] * n_in,
            out_specs=[token_spec(width), token_spec(width), token_spec(128)] + grad_specs,
            scratch_shapes=[
                pltpu.VMEM((kinds, width, hidden), BF16),
                pltpu.VMEM((kinds, width, hidden), F32),
                pltpu.VMEM((tokens, width), F32),
                pltpu.VMEM((tokens, width), F32),
            ],
        ),
        out_shape=[
            jax.ShapeDtypeStruct((tokens, width), BF16),
            jax.ShapeDtypeStruct((tokens, width), BF16),
            jax.ShapeDtypeStruct((tokens, 128), F32),
        ]
        + grad_shapes,
        compiler_params=pltpu.CompilerParams(vmem_limit_bytes=60 << 20),
        cost_estimate=pl.CostEstimate(
            flops=group * slots * width * (18 * hidden + 8 * tokens),
            bytes_accessed=16 * tokens * width,
            transcendentals=0,
        ),
    )(counts, place, rows, grads, slot_rows, gate_rows, slot_cols, gate_cols, *pieces)


def per_device(
    tokens_in,
    carried_logits,
    cotangent,
    segment_ids,
    parent_ids,
    routes,
    attention_gain,
    head_weight,
    output_weight,
    expert_gain,
    router_weight,
    carry_weight,
    constant_gate,
    constant_vector,
    expert_first,
    expert_second,
):
    row_count, width = tokens_in.shape
    tree_len = segment_ids.shape[0]
    head_width = head_weight.shape[2]
    heads = head_width // HEAD
    share = head_weight.shape[1]
    group = NF // GROUPS
    me = lax.axis_index("dp")
    place = me ^ jnp.arange(8, dtype=jnp.int32)

    by_section = jnp.concatenate([head_weight, output_weight.T[None]], axis=0).astype(BF16)
    by_section = jnp.pad(by_section, ((0, 0), (0, 0), (0, PAD - head_width)))
    head_pack = by_section.transpose(1, 0, 2).reshape(share, 4 * PAD)
    expert_pack = jnp.concatenate(
        [expert_first.astype(BF16), expert_second.astype(BF16).transpose(0, 2, 1)[:, None]], axis=1
    )

    token_values = tokens_in.astype(F32)
    normed_one = normed(token_values, attention_gain).astype(BF16)
    gathered_one = gather_tensor(normed_one)
    head_pieces = pieces_of(head_pack, 0)
    if len(head_pieces) == 1:
        head_full = head_pieces[0]
    else:
        stacked = jnp.zeros((len(head_pieces), share, 4 * PAD), BF16)
        for k, piece in enumerate(head_pieces):
            stacked = lax.dynamic_update_slice(stacked, piece[None], (place[k], 0, 0))
        head_full = stacked.reshape(width, 4 * PAD)
    expert_pieces = [
        pieces_of(expert_pack[g * group : (g + 1) * group], 2) for g in range(GROUPS)
    ]
    gathered_grads = gather_tensor(cotangent)

    hot = jnp.sum((routes[:, :, None] == jnp.arange(NF, dtype=jnp.int32)).astype(jnp.int32), axis=1)
    rank = jnp.cumsum(hot, axis=0) - hot
    counts = jnp.sum(hot, axis=0)
    slot_cols = jnp.where(hot > 0, rank, -1)
    slot_rows = slot_cols.T[:, None, :]

    cos_table, sin_table = rotary_tables(segment_ids, parent_ids)
    rowinfo = jnp.pad(jnp.stack([segment_ids, parent_ids]), ((0, 6), (0, 0)))
    colinfo = rowinfo.T
    queries, keys, values, keys_t, values_t = project(gathered_one, head_full, cos_table, sin_table)
    attended, totals = attend(heads, queries, keys, values_t, rowinfo, colinfo)
    output_full = head_full[:, 3 * PAD :]
    attention_part = dot_nt(attended, output_full)
    hidden = token_values + scatter_tensor(attention_part, row_count)

    local_routes = lax.dynamic_slice_in_dim(
        routes, lax.axis_index("tensor") * row_count, row_count, 0
    )
    (normed_two, gates, local_sum), pull_router = jax.vjp(
        functools.partial(router_local, routes=local_routes),
        hidden,
        expert_gain,
        carried_logits,
        router_weight,
        carry_weight,
        constant_gate,
        constant_vector,
    )
    gathered_two = gather_tensor(normed_two.astype(BF16))
    gate_cols = gather_tensor(gates.astype(BF16)).astype(F32)
    gate_rows = gate_cols.T[:, None, :]

    sums, grad_ins, gate_grads, own_grads = [], [], [], []
    for g in range(GROUPS):
        part, grad_in, gate_grad, *grad_pieces = experts(
            g * group, expert_pieces[g], counts, place, gathered_two, gathered_grads,
            slot_rows, gate_rows, slot_cols, gate_cols,
        )
        sums.append(part.astype(F32))
        grad_ins.append(grad_in.astype(F32))
        gate_grads.append(gate_grad)
        if len(grad_pieces) == 1:
            own_grads.append(
                lax.psum_scatter(grad_pieces[0].astype(F32), "dp", scatter_dimension=2, tiled=True)
            )
        else:
            own_grads.append(sum_pieces(*grad_pieces))
    grad_normed_two = scatter_tensor(sum(grad_ins), row_count)
    grad_gates = lax.psum_scatter(
        sum(gate_grads)[:, :NF], "tensor", scatter_dimension=0, tiled=True
    )
    expert_total = scatter_tensor(sum(sums), row_count)
    output = (hidden + local_sum + expert_total).astype(BF16)
    own_grads = jnp.concatenate(own_grads, axis=0)
    grad_first = own_grads[:, :2]
    grad_second = own_grads[:, 2].transpose(0, 2, 1)

    grad_values_out = cotangent.astype(F32)
    (
        grad_hidden_local,
        grad_expert_gain,
        grad_carried,
        grad_router,
        grad_carry,
        grad_constant_gate,
        grad_constant_vector,
    ) = pull_router((grad_normed_two, grad_gates, grad_values_out))
    grad_hidden = grad_values_out + grad_hidden_local
    small = [grad_expert_gain, grad_router, grad_carry, grad_constant_gate, grad_constant_vector]
    flat = sum_all(jnp.concatenate([s.reshape(-1) for s in small]))
    small_out, at = [], 0
    for s in small:
        small_out.append(flat[at : at + s.size].reshape(s.shape))
        at += s.size

    grad_branch = gather_tensor(grad_hidden.astype(BF16))
    grad_attended = dot_nn(grad_branch, output_full).astype(BF16)
    grad_output_t = dot_tn(grad_branch, attended)
    grad_projected = jnp.concatenate(
        attend_back(
            heads, queries, grad_attended, attended, keys, values, keys_t, rowinfo, colinfo, totals,
            cos_table, sin_table,
        ),
        axis=1,
    )
    grad_head = dot_tn(gathered_one, grad_projected)
    grad_normed_all = dot_nt(grad_projected, head_full[:, : 3 * PAD])
    grad_normed_one = scatter_tensor(grad_normed_all, row_count)
    grad_pack = jnp.concatenate([grad_head, grad_output_t], axis=1).astype(BF16)
    if len(head_pieces) == 1:
        own_pack = lax.psum_scatter(grad_pack.astype(F32), "dp", scatter_dimension=0, tiled=True)
    else:
        blocks = grad_pack.reshape(8, share, 4 * PAD)
        ordered = [lax.dynamic_index_in_dim(blocks, place[k], 0, keepdims=False) for k in range(8)]
        own_pack = sum_pieces(jnp.stack(ordered[0::2]), jnp.stack(ordered[1::2]))
    own_pack = own_pack.reshape(share, 4, PAD)[:, :, :head_width].transpose(1, 0, 2)
    grad_head_own = own_pack[:3]
    grad_output_own = own_pack[3].T

    norm_values, pull_norm = jax.vjp(normed, token_values, attention_gain)
    grad_token_part, grad_attention_gain = pull_norm(grad_normed_one)
    grad_tokens = grad_hidden + grad_token_part
    grad_attention_gain = sum_all(grad_attention_gain)
    return (
        output,
        grad_tokens,
        grad_carried,
        grad_attention_gain,
        grad_head_own,
        grad_output_own,
        *small_out,
        grad_first,
        grad_second,
    )


def solution(mesh):
    in_specs = (
        P(("dp", "tensor"), None),
        P(("dp", "tensor"), None),
        P(("dp", "tensor"), None),
        P("dp"),
        P("dp"),
        P("dp", None),
        P(),
        P(None, "dp", "tensor"),
        P("tensor", "dp"),
        P(),
        P(),
        P(),
        P(),
        P(),
        P(None, None, "dp", "tensor"),
        P(None, "tensor", "dp"),
    )
    out_specs = (
        P(("dp", "tensor"), None),
        P(("dp", "tensor"), None),
        P(("dp", "tensor"), None),
        P(),
        P(None, "dp", "tensor"),
        P("tensor", "dp"),
        P(),
        P(),
        P(),
        P(),
        P(),
        P(None, None, "dp", "tensor"),
        P(None, "tensor", "dp"),
    )
    return jax.shard_map(
        per_device, mesh=mesh, in_specs=in_specs, out_specs=out_specs, check_vma=False
    )
```

time: 1880 us -> 916 us (0.49)
  waiting for transfers between devices: 995 us -> 276 us
  matrix products: 279 us -> 28 us
  Pallas kernels: 0 us -> 224 us
  starting transfers between devices: 1.04 us -> 169 us
  local copies, waits for them, and re-layouts: 218 us -> 58.5 us
  blocking collectives: 122 us -> 0 us
  other arithmetic: 234 us -> 117 us
    reduce_scatter x7 -> x1, waiting for transfers between devices: 715 us -> 0.01 us  [per_device(): lax.psum_scatter(sum(gate_grads)[:, :NF], 'tensor', scatter_dimension=0,...]
    ppermute x0 -> x88, waiting for transfers between devices: none -> 276 us  [swap(): return lax.ppermute(values, axis, [(i, i ^ bits) for i in range(size)])]
    dot_general x40 -> x5, matrix products: 254 us -> 14.6 us  [the longest x1 5.71 us: dot_nn(): lax.dot_general(a, b, (((1,), (0,)), ((), ())), preferred_element_type=F32)]
    all_gather x6 -> x0, waiting for transfers between devices: 228 us -> none  [the longest x1 123 us: per_device(): lax.all_gather(first_low, 'dp', axis=2, tiled=True)]
    pallas_call x0 -> x7, Pallas kernels: none -> 224 us  [the longest x4 135 us: experts(): pl.pallas_call(functools.partial(experts_kernel, first, n_in, len(grad_sp...]
    ppermute x0 -> x88, starting transfers between devices: none -> 169 us  [swap(): return lax.ppermute(values, axis, [(i, i ^ bits) for i in range(size)])]
    scatter-add x3 -> x0, other arithmetic: 89.3 us -> none  [the longest x1 31.3 us: per_device(): expert_partial = jnp.zeros((tree_len, width), jnp.float32).at[token_index...]
    all_gather x3 -> x0, blocking collectives: 76.5 us -> none  [the longest x1 38.6 us: per_device(): lax.all_gather(head_low, 'dp', axis=1, tiled=True)]
  transfers between devices with their start and end apart: 15 -> 89, of which waited for: 11 -> 27; matrix products, arithmetic and copies ran while one was open for 16% -> 20% of each run, Pallas kernels for 0% -> 25%
where the time goes in v1:
time: 916 us; the launch traced here: 905 us
  waiting for transfers between devices  276 us (30%)
  Pallas kernels  224 us (24%)
  starting transfers between devices  169 us (18%)
  other arithmetic  117 us (13%)
  local copies, waits for them, and re-layouts  58.5 us (6%)
  between operations  31.8 us (3%)
  matrix products  28 us (3%)
    ppermute x88, waiting for transfers between devices, swap(): return lax.ppermute(values, axis, [(i, i ^ bits) for i in range(size)])  276 us
    ppermute x88, starting transfers between devices, swap(): return lax.ppermute(values, axis, [(i, i ^ bits) for i in range(size)])  169 us
    pallas_call x4, Pallas kernels, experts(): pl.pallas_call(functools.partial(experts_kernel, first, n_in, len(grad_sp...  135 us
    pallas_call x1, Pallas kernels, attend_back(): pl.pallas_call(functools.partial(attend_back_kernel, heads), grid=(rows /...  54 us
    pallas_call x1, Pallas kernels, attend(): pl.pallas_call(functools.partial(attend_kernel, heads), grid=(rows // BLO...  24.7 us
    another operation x10, other arithmetic  23.6 us
    unnamed x154, local copies, waits for them, and re-layouts  20.9 us
  transfers between devices with their start and end apart: 89, of which 27 were waited for; matrix products, arithmetic and copies ran while one was open for 20% of the time, Pallas kernels for 25%

profile of v1, /device:TPU:0, one launch (start us, length us, event | category | flops | bytes accessed | tf_op | source)
XLA Modules:
  0.0 904.5 jit_solution(14319764672212560708)
XLA Ops:
  11.0 2.9 collective-permute-start.1
  41.1 2.9 copy.170.c_ref
  59.6 3.7 collective-permute-done.5
  65.4 3.7 collective-permute-done.7
  69.7 5.1 collective-permute-done.9
  75.4 3.6 collective-permute-start.24
  83.6 10.2 %shard_map.255 = (bf16[2048,256]{1,0:T(8,128)(2,1)}, bf16[2048,256]{1,0:T(8,128)(2,1)}, bf16[2048,256]{1,0:T(8,128)(2,1)}, bf16[256,2048]{1,0:T(8,128)(2,1)}, bf16[256,2048]{1,0:T(8,128)(2,1)}) custom-call(bf16[2048,768]{1,0:T(8,128)(2,1)} %pad_maximum_fusion.1.n_ref, bf16[768,1024]{1,0:T(8,128)(2,1)} %bitcast.197, f32[2048,256]{1,0:T(8,128)} %copy.170.c_ref, ...), custom_call_target="tpu_custom_call" | custom-call | flops 2415919104 | bytes 12582912 | tf_op jit(solution)/shard_map/pallas_call | solution.py:187
  97.5 24.7 %shard_map.256 = (bf16[2048,256]{1,0:T(8,128)(2,1)S(1)}, f32[8,2048]{1,0:T(8,128)S(1)}) custom-call(bf16[2048,256]{1,0:T(8,128)(2,1)S(1)} %copy-done.4, bf16[2048,256]{1,0:T(8,128)(2,1)S(1)} %copy-done.6, bf16[256,2048]{1,0:T(8,128)(2,1)S(1)} %copy-done.10, s32[8,2048]{1,0:T(8,128)S(1)} %pad.39.clone.rowinfo_ref, s32[2048,8]{1,0:T(8,128)S(1)} %pad_bitcast_fusion.colinfo_ref), custom_call_target="tpu_custom_call" | custom-call | flops 6442450944 | bytes 4194304 | tf_op jit(solution)/shard_map/pallas_call | solution.py:259
  146.5 14.3 %collective-permute-done.11 = bf16[512,768]{1,0:T(8,128)(2,1)S(1)} collective-permute-done((bf16[512,768]{1,0:T(8,128)(2,1)S(1)}, bf16[512,768]{1,0:T(8,128)(2,1)S(1)}, u32[]{:S(2)}, u32[]{:S(2)}) %collective-permute-start.11) | collective-permute-done | bytes 786464 | tf_op jit(solution)/shard_map/ppermute | solution.py:102
  170.9 13.7 %collective-permute-done.19 = bf16[512,8]{0,1:T(8,128)(2,1)S(1)} collective-permute-done((bf16[512,8]{0,1:T(8,128)(2,1)S(1)}, bf16[512,8]{0,1:T(8,128)(2,1)S(1)}, u32[]{:S(2)}, u32[]{:S(2)}) %collective-permute-start.19) | collective-permute-done | bytes 8224 | tf_op jit(solution)/shard_map/ppermute | solution.py:102
  187.9 9.3 %collective-permute-done.29.refs_2_ = bf16[2,3,96,512]{3,2,1,0:T(8,128)(2,1)} collective-permute-done((bf16[2,3,96,512]{3,2,1,0:T(8,128)(2,1)}, bf16[2,3,96,512]{3,2,1,0:T(8,128)(2,1)}, u32[]{:S(2)}, u32[]{:S(2)}) %collective-permute-start.29) | collective-permute-done | bytes 589856 | tf_op jit(solution)/shard_map/ppermute | solution.py:102
  198.7 11.6 %collective-permute-done.31.refs_4_ = bf16[2,3,96,512]{3,2,1,0:T(8,128)(2,1)} collective-permute-done((bf16[2,3,96,512]{3,2,1,0:T(8,128)(2,1)}, bf16[2,3,96,512]{3,2,1,0:T(8,128)(2,1)}, u32[]{:S(2)}, u32[]{:S(2)}) %collective-permute-start.31) | collective-permute-done | bytes 589856 | tf_op jit(solution)/shard_map/ppermute | solution.py:102
  214.3 9.4 %collective-permute-start.38 = (bf16[2,3,96,512]{3,2,1,0:T(8,128)(2,1)}, bf16[2,3,96,512]{3,2,1,0:T(8,128)(2,1)S(1)}, u32[]{:S(2)}, u32[]{:S(2)}) collective-permute-start(bf16[2,3,96,512]{3,2,1,0:T(8,128)(2,1)} %get-tuple-element.206.refs_0_), channel_id=1, source_target_pairs={{0,16},{4,20},{8,24},{12,28},{16,0},{20,4},{24,8},{28,12},{1,17},{... | collective-permute-start | bytes 1769480 | tf_op jit(solution)/shard_map/ppermute | solution.py:102
  233.2 30.1 %collective-permute-done.38.refs_4_ = bf16[2,3,96,512]{3,2,1,0:T(8,128)(2,1)S(1)} collective-permute-done((bf16[2,3,96,512]{3,2,1,0:T(8,128)(2,1)}, bf16[2,3,96,512]{3,2,1,0:T(8,128)(2,1)S(1)}, u32[]{:S(2)}, u32[]{:S(2)}) %collective-permute-start.38) | collective-permute-done | bytes 589856 | tf_op jit(solution)/shard_map/ppermute | solution.py:102
  265.7 10.6 %collective-permute-start.43 = (bf16[2,3,96,512]{3,2,1,0:T(8,128)(2,1)S(1)}, bf16[2,3,96,512]{3,2,1,0:T(8,128)(2,1)}, u32[]{:S(2)}, u32[]{:S(2)}) collective-permute-start(bf16[2,3,96,512]{3,2,1,0:T(8,128)(2,1)S(1)} %copy-done.53), channel_id=1, source_target_pairs={{0,8},{4,12},{8,0},{12,4},{16,24},{20,28},{24,16},{28,20},{1,9},{5... | collective-permute-start | bytes 1769480 | tf_op jit(solution)/shard_map/ppermute | solution.py:102
  279.9 36.3 %shard_map.257 = (bf16[2048,768]{1,0:T(8,128)(2,1)}, bf16[2048,768]{1,0:T(8,128)(2,1)}, f32[2048,128]{1,0:T(8,128)}, bf16[4,2,3,96,512]{4,3,2,1,0:T(8,128)(2,1)}, bf16[4,2,3,96,512]{4,3,2,1,0:T(8,128)(2,1)}) custom-call(s32[8]{0:T(128)} %get-tuple-element.152.counts_ref, s32[8]{0:T(128)} %copy-done.66, bf16[2048,768]{1,0:T(8,128)(2,1)} %pad_maximum_fusion.2.rows_ref, ...), custom_call_target="tpu_custom_call" | custom-call | flops 20132659200 | bytes 25165824 | tf_op jit(solution)/shard_map/pallas_call | solution.py:499
  321.3 25.0 %shard_map.258 = (bf16[2048,768]{1,0:T(8,128)(2,1)}, bf16[2048,768]{1,0:T(8,128)(2,1)}, f32[2048,128]{1,0:T(8,128)}, bf16[4,2,3,96,512]{4,3,2,1,0:T(8,128)(2,1)}, bf16[4,2,3,96,512]{4,3,2,1,0:T(8,128)(2,1)}) custom-call(s32[8]{0:T(128)} %get-tuple-element.152.counts_ref, s32[8]{0:T(128)} %copy-done.66, bf16[2048,768]{1,0:T(8,128)(2,1)} %pad_maximum_fusion.2.rows_ref, ...), custom_call_target="tpu_custom_call" | custom-call | flops 20132659200 | bytes 25165824 | tf_op jit(solution)/shard_map/pallas_call | solution.py:499
  346.3 8.4 collective-permute-done.45.refs_4_
  360.3 36.5 %shard_map.259 = (bf16[2048,768]{1,0:T(8,128)(2,1)}, bf16[2048,768]{1,0:T(8,128)(2,1)}, f32[2048,128]{1,0:T(8,128)}, bf16[4,2,3,96,512]{4,3,2,1,0:T(8,128)(2,1)}, bf16[4,2,3,96,512]{4,3,2,1,0:T(8,128)(2,1)}) custom-call(s32[8]{0:T(128)} %get-tuple-element.152.counts_ref, s32[8]{0:T(128)} %copy-done.66, bf16[2048,768]{1,0:T(8,128)(2,1)} %pad_maximum_fusion.2.rows_ref, ...), custom_call_target="tpu_custom_call" | custom-call | flops 20132659200 | bytes 25165824 | tf_op jit(solution)/shard_map/pallas_call | solution.py:499
  396.9 12.0 %collective-permute-done.48.refs_7_ = bf16[2,3,96,512]{3,2,1,0:T(8,128)(2,1)} collective-permute-done((bf16[2,3,96,512]{3,2,1,0:T(8,128)(2,1)}, bf16[2,3,96,512]{3,2,1,0:T(8,128)(2,1)}, u32[]{:S(2)}, u32[]{:S(2)}) %collective-permute-start.48) | collective-permute-done | bytes 589856 | tf_op jit(solution)/shard_map/ppermute | solution.py:102
  408.9 36.9 %shard_map.260 = (bf16[2048,768]{1,0:T(8,128)(2,1)}, bf16[2048,768]{1,0:T(8,128)(2,1)}, f32[2048,128]{1,0:T(8,128)}, bf16[4,2,3,96,512]{4,3,2,1,0:T(8,128)(2,1)}, bf16[4,2,3,96,512]{4,3,2,1,0:T(8,128)(2,1)}) custom-call(s32[8]{0:T(128)} %get-tuple-element.152.counts_ref, s32[8]{0:T(128)} %copy-done.66, bf16[2048,768]{1,0:T(8,128)(2,1)} %pad_maximum_fusion.2.rows_ref, ...), custom_call_target="tpu_custom_call" | custom-call | flops 20132659200 | bytes 25165824 | tf_op jit(solution)/shard_map/pallas_call | solution.py:499
  445.9 6.2 convert_add_fusion.1
  457.7 3.5 convert_add_fusion
  476.3 3.6 fusion.32
  481.1 4.8 fusion.86
  487.2 12.6 %collective-permute-done.50 = bf16[512,768]{1,0:T(8,128)(2,1)S(1)} collective-permute-done((bf16[512,768]{1,0:T(8,128)(2,1)S(1)}, bf16[512,768]{1,0:T(8,128)(2,1)S(1)}, u32[]{:S(2)}, u32[]{:S(2)}) %collective-permute-start.50) | collective-permute-done | bytes 786464 | tf_op jit(solution)/shard_map/ppermute | solution.py:102
  499.8 5.1 fusion.23
  512.2 3.5 fusion.93
  520.6 4.0 multiply_reduce_fusion
  524.7 4.4 collective-permute-start.75
  529.1 5.8 fusion.87
  534.9 35.5 %collective-permute-done.80 = bf16[4,2,3,96,512]{4,3,2,1,0:T(8,128)(2,1)} collective-permute-done((bf16[4,2,3,96,512]{4,3,2,1,0:T(8,128)(2,1)}, bf16[4,2,3,96,512]{4,3,2,1,0:T(8,128)(2,1)}, u32[]{:S(2)}, u32[]{:S(2)}) %collective-permute-start.80) | collective-permute-done | bytes 2359328 | tf_op jit(solution)/shard_map/ppermute | solution.py:102
  570.4 4.9 fusion.88
  579.8 40.7 %collective-permute-done.84 = bf16[4,2,3,96,512]{4,3,2,1,0:T(8,128)(2,1)} collective-permute-done((bf16[4,2,3,96,512]{4,3,2,1,0:T(8,128)(2,1)}, bf16[4,2,3,96,512]{4,3,2,1,0:T(8,128)(2,1)}, u32[]{:S(2)}, u32[]{:S(2)}) %collective-permute-start.84) | collective-permute-done | bytes 2359328 | tf_op jit(solution)/shard_map/ppermute | solution.py:102
  622.1 5.0 fusion.89
  627.2 4.2 collective-permute-done.70
  649.0 26.3 %collective-permute-done.78 = bf16[2,3,96,512]{3,2,1,0:T(8,128)(2,1)} collective-permute-done((bf16[2,3,96,512]{3,2,1,0:T(8,128)(2,1)}, bf16[2,3,96,512]{3,2,1,0:T(8,128)(2,1)}, u32[]{:S(2)}, u32[]{:S(2)}) %collective-permute-start.78) | collective-permute-done | bytes 589856 | tf_op jit(solution)/shard_map/ppermute | solution.py:102
  682.0 5.5 collective-permute-done.81
  687.4 32.2 %collective-permute-start.85 = (bf16[2,3,96,512]{3,2,1,0:T(8,128)(2,1)}, bf16[2,3,96,512]{3,2,1,0:T(8,128)(2,1)}, u32[]{:S(2)}, u32[]{:S(2)}) collective-permute-start(bf16[2,3,96,512]{3,2,1,0:T(8,128)(2,1)} %get-tuple-element.200), channel_id=1, source_target_pairs={{0,8},{4,12},{8,0},{12,4},{16,24},{20,28},{24,16},{28,20},{1,9},{5... | collective-permute-start | bytes 1769480 | tf_op jit(solution)/shard_map/ppermute | solution.py:102
  719.6 6.3 collective-permute-done.82
  731.7 5.7 convolution_convert_fusion.g_ref
  737.6 54.0 %shard_map.261 = (bf16[2048,256]{1,0:T(8,128)(2,1)S(1)}, bf16[2048,256]{1,0:T(8,128)(2,1)S(1)}, bf16[2048,256]{1,0:T(8,128)(2,1)S(1)}) custom-call(bf16[2048,256]{1,0:T(8,128)(2,1)S(1)} %copy-done.5, bf16[2048,256]{1,0:T(8,128)(2,1)S(1)} %convolution_convert_fusion.g_ref, bf16[2048,256]{1,0:T(8,128)(2,1)S(1)} %copy-done.2, bf16[2048,256]{1,0:T(8,128)(2,1)S(1)} %copy-done.7, ...), custom_call_target="tpu_custom_call" | custom-call | flops 16106127360 | bytes 8388608 | tf_op jit(solution)/shard_map/pallas_call | solution.py:369
  811.9 9.4 %collective-permute-done.63 = bf16[4,96,1024]{2,1,0:T(8,128)(2,1)S(1)} collective-permute-done((bf16[4,96,1024]{2,1,0:T(8,128)(2,1)S(1)}, bf16[4,96,1024]{2,1,0:T(8,128)(2,1)S(1)}, u32[]{:S(2)}, u32[]{:S(2)}) %collective-permute-start.63) | collective-permute-done | bytes 786464 | tf_op jit(solution)/shard_map/ppermute | solution.py:102
  821.8 37.6 %collective-permute-start.64 = (bf16[96,1024]{1,0:T(8,128)(2,1)S(1)}, bf16[96,1024]{1,0:T(8,128)(2,1)S(1)}, u32[]{:S(2)}, u32[]{:S(2)}) collective-permute-start(bf16[96,1024]{1,0:T(8,128)(2,1)S(1)} %get-tuple-element.218), channel_id=1, source_target_pairs={{0,8},{4,12},{8,0},{12,4},{16,24},{20,28},{24,16},{28,20},{1,9},{5... | collective-permute-start | bytes 589832 | tf_op jit(solution)/shard_map/ppermute | solution.py:102
  861.9 3.0 fusion.12
  865.3 10.3 %collective-permute-done.65 = bf16[96,1024]{1,0:T(8,128)(2,1)S(1)} collective-permute-done((bf16[96,1024]{1,0:T(8,128)(2,1)S(1)}, bf16[96,1024]{1,0:T(8,128)(2,1)S(1)}, u32[]{:S(2)}, u32[]{:S(2)}) %collective-permute-start.65) | collective-permute-done | bytes 196640 | tf_op jit(solution)/shard_map/ppermute | solution.py:102
  889.2 3.4 collective-permute-start.62
  892.6 4.0 fusion.13
  (484 shorter events, 220.0 us)
Async XLA Ops:
  7.2 499.0 %reduce-scatter.2.cloned.1.call-start = ((), (), s32[]{:S(2)}) async-start(), calls=%async_computation.1 | async-start | bytes 1310720 | tf_op jit(solution)/shard_map/reduce_scatter | solution.py:627
  11.0 52.8 %collective-permute-start.1 = (bf16[512,768]{1,0:T(8,128)(2,1)}, bf16[512,768]{1,0:T(8,128)(2,1)}, u32[]{:S(2)}, u32[]{:S(2)}) collective-permute-start(bf16[512,768]{1,0:T(8,128)(2,1)} %fusion.11), channel_id=1, source_target_pairs={{0,2},{1,3},{2,0},{3,1},{4,6},{5,7},{6,4},{7,5},{8,10},{9,11},{10,... | collective-permute-start | bytes 2359304 | tf_op jit(solution)/shard_map/ppermute | solution.py:102
  13.9 61.4 %collective-permute-start = (bf16[512,768]{1,0:T(8,128)(2,1)}, bf16[512,768]{1,0:T(8,128)(2,1)}, u32[]{:S(2)}, u32[]{:S(2)}) collective-permute-start(bf16[512,768]{1,0:T(8,128)(2,1)} %fusion.11), channel_id=1, source_target_pairs={{0,1},{1,0},{2,3},{3,2},{4,5},{5,4},{6,7},{7,6},{8,9},{9,8},{10,11... | collective-permute-start | bytes 2359304 | tf_op jit(solution)/shard_map/ppermute | solution.py:102
  14.2 42.2 %collective-permute-start.3 = (bf16[96,1024]{1,0:T(8,128)(2,1)S(1)}, bf16[96,1024]{1,0:T(8,128)(2,1)}, u32[]{:S(2)}, u32[]{:S(2)}) collective-permute-start(bf16[96,1024]{1,0:T(8,128)(2,1)S(1)} %bitcast.204), channel_id=1, source_target_pairs={{0,4},{4,0},{8,12},{12,8},{16,20},{20,16},{24,28},{28,24},{1,5},{5... | collective-permute-start | bytes 589832 | tf_op jit(solution)/shard_map/ppermute | solution.py:102
  15.8 40.9 %collective-permute-start.4 = (bf16[96,1024]{1,0:T(8,128)(2,1)S(1)}, bf16[96,1024]{1,0:T(8,128)(2,1)}, u32[]{:S(2)}, u32[]{:S(2)}) collective-permute-start(bf16[96,1024]{1,0:T(8,128)(2,1)S(1)} %bitcast.205), channel_id=1, source_target_pairs={{0,8},{4,12},{8,0},{12,4},{16,24},{20,28},{24,16},{28,20},{1,9},{5... | collective-permute-start | bytes 589832 | tf_op jit(solution)/shard_map/ppermute | solution.py:102
  17.3 41.8 %collective-permute-start.6 = (bf16[96,1024]{1,0:T(8,128)(2,1)S(1)}, bf16[96,1024]{1,0:T(8,128)(2,1)}, u32[]{:S(2)}, u32[]{:S(2)}) collective-permute-start(bf16[96,1024]{1,0:T(8,128)(2,1)S(1)} %bitcast.206), channel_id=1, source_target_pairs={{0,16},{4,20},{8,24},{12,28},{16,0},{20,4},{24,8},{28,12},{1,17},{... | collective-permute-start | bytes 589832 | tf_op jit(solution)/shard_map/ppermute | solution.py:102
  59.1 75.9 %collective-permute-start.16 = (bf16[512,768]{1,0:T(8,128)(2,1)}, bf16[512,768]{1,0:T(8,128)(2,1)}, u32[]{:S(2)}, u32[]{:S(2)}) collective-permute-start(bf16[512,768]{1,0:T(8,128)(2,1)} %param.18), channel_id=1, source_target_pairs={{0,2},{1,3},{2,0},{3,1},{4,6},{5,7},{6,4},{7,5},{8,10},{9,11},{10,... | collective-permute-start | bytes 2359304 | tf_op jit(solution)/shard_map/ppermute | solution.py:102
  64.9 77.0 %collective-permute-start.15 = (bf16[512,768]{1,0:T(8,128)(2,1)}, bf16[512,768]{1,0:T(8,128)(2,1)}, u32[]{:S(2)}, u32[]{:S(2)}) collective-permute-start(bf16[512,768]{1,0:T(8,128)(2,1)} %param.18), channel_id=1, source_target_pairs={{0,1},{1,0},{2,3},{3,2},{4,5},{5,4},{6,7},{7,6},{8,9},{9,8},{10,11... | collective-permute-start | bytes 2359304 | tf_op jit(solution)/shard_map/ppermute | solution.py:102
  74.8 94.6 %collective-permute-start.22 = (bf16[2,3,96,512]{3,2,1,0:T(8,128)(2,1)}, bf16[2,3,96,512]{3,2,1,0:T(8,128)(2,1)}, u32[]{:S(2)}, u32[]{:S(2)}) collective-permute-start(bf16[2,3,96,512]{3,2,1,0:T(8,128)(2,1)} %get-tuple-element.203.refs_0_), channel_id=1, source_target_pairs={{0,8},{4,12},{8,0},{12,4},{16,24},{20,28},{24,16},{28,20},{1,9},{5... | collective-permute-start | bytes 1769480 | tf_op jit(solution)/shard_map/ppermute | solution.py:102
  75.4 94.6 %collective-permute-start.24 = (bf16[2,3,96,512]{3,2,1,0:T(8,128)(2,1)}, bf16[2,3,96,512]{3,2,1,0:T(8,128)(2,1)}, u32[]{:S(2)}, u32[]{:S(2)}) collective-permute-start(bf16[2,3,96,512]{3,2,1,0:T(8,128)(2,1)} %get-tuple-element.203.refs_0_), channel_id=1, source_target_pairs={{0,16},{4,20},{8,24},{12,28},{16,0},{20,4},{24,8},{28,12},{1,17},{... | collective-permute-start | bytes 1769480 | tf_op jit(solution)/shard_map/ppermute | solution.py:102
  170.0 40.3 %collective-permute-start.31 = (bf16[2,3,96,512]{3,2,1,0:T(8,128)(2,1)}, bf16[2,3,96,512]{3,2,1,0:T(8,128)(2,1)}, u32[]{:S(2)}, u32[]{:S(2)}) collective-permute-start(bf16[2,3,96,512]{3,2,1,0:T(8,128)(2,1)} %get-tuple-element.204.refs_0_), channel_id=1, source_target_pairs={{0,16},{4,20},{8,24},{12,28},{16,0},{20,4},{24,8},{28,12},{1,17},{... | collective-permute-start | bytes 1769480 | tf_op jit(solution)/shard_map/ppermute | solution.py:102
  187.0 40.4 %collective-permute-start.12 = (bf16[512,768]{1,0:T(8,128)(2,1)}, bf16[512,768]{1,0:T(8,128)(2,1)}, u32[]{:S(2)}, u32[]{:S(2)}) collective-permute-start(bf16[512,768]{1,0:T(8,128)(2,1)} %fusion.94), channel_id=1, source_target_pairs={{0,1},{1,0},{2,3},{3,2},{4,5},{5,4},{6,7},{7,6},{8,9},{9,8},{10,11... | collective-permute-start | bytes 2359304 | tf_op jit(solution)/shard_map/ppermute | solution.py:102
  187.1 40.7 %collective-permute-start.14 = (bf16[512,768]{1,0:T(8,128)(2,1)}, bf16[512,768]{1,0:T(8,128)(2,1)}, u32[]{:S(2)}, u32[]{:S(2)}) collective-permute-start(bf16[512,768]{1,0:T(8,128)(2,1)} %collective-permute-done.13), channel_id=1, source_target_pairs={{0,1},{1,0},{2,3},{3,2},{4,5},{5,4},{6,7},{7,6},{8,9},{9,8},{10,11... | collective-permute-start | bytes 2359304 | tf_op jit(solution)/shard_map/ppermute | solution.py:102
  214.3 49.1 %collective-permute-start.38 = (bf16[2,3,96,512]{3,2,1,0:T(8,128)(2,1)}, bf16[2,3,96,512]{3,2,1,0:T(8,128)(2,1)S(1)}, u32[]{:S(2)}, u32[]{:S(2)}) collective-permute-start(bf16[2,3,96,512]{3,2,1,0:T(8,128)(2,1)} %get-tuple-element.206.refs_0_), channel_id=1, source_target_pairs={{0,16},{4,20},{8,24},{12,28},{16,0},{20,4},{24,8},{28,12},{1,17},{... | collective-permute-start | bytes 1769480 | tf_op jit(solution)/shard_map/ppermute | solution.py:102
  223.7 41.2 %collective-permute-start.40 = (bf16[2,3,96,512]{3,2,1,0:T(8,128)(2,1)}, bf16[2,3,96,512]{3,2,1,0:T(8,128)(2,1)S(1)}, u32[]{:S(2)}, u32[]{:S(2)}) collective-permute-start(bf16[2,3,96,512]{3,2,1,0:T(8,128)(2,1)} %get-tuple-element.206.refs_0_), channel_id=1, source_target_pairs={{0,24},{4,28},{8,16},{12,20},{16,8},{20,12},{24,0},{28,4},{1,25},{... | collective-permute-start | bytes 1769480 | tf_op jit(solution)/shard_map/ppermute | solution.py:102
  225.8 50.5 %collective-permute-start.23 = (bf16[2,3,96,512]{3,2,1,0:T(8,128)(2,1)}, bf16[2,3,96,512]{3,2,1,0:T(8,128)(2,1)}, u32[]{:S(2)}, u32[]{:S(2)}) collective-permute-start(bf16[2,3,96,512]{3,2,1,0:T(8,128)(2,1)} %collective-permute-done.22.refs_2_), channel_id=1, source_target_pairs={{0,4},{4,0},{8,12},{12,8},{16,20},{20,16},{24,28},{28,24},{1,5},{5... | collective-permute-start | bytes 1769480 | tf_op jit(solution)/shard_map/ppermute | solution.py:102
  227.3 50.5 %collective-permute-start.25 = (bf16[2,3,96,512]{3,2,1,0:T(8,128)(2,1)}, bf16[2,3,96,512]{3,2,1,0:T(8,128)(2,1)}, u32[]{:S(2)}, u32[]{:S(2)}) collective-permute-start(bf16[2,3,96,512]{3,2,1,0:T(8,128)(2,1)} %collective-permute-done.24.refs_4_), channel_id=1, source_target_pairs={{0,4},{4,0},{8,12},{12,8},{16,20},{20,16},{24,28},{28,24},{1,5},{5... | collective-permute-start | bytes 1769480 | tf_op jit(solution)/shard_map/ppermute | solution.py:102
  227.8 50.5 %collective-permute-start.27 = (bf16[2,3,96,512]{3,2,1,0:T(8,128)(2,1)}, bf16[2,3,96,512]{3,2,1,0:T(8,128)(2,1)}, u32[]{:S(2)}, u32[]{:S(2)}) collective-permute-start(bf16[2,3,96,512]{3,2,1,0:T(8,128)(2,1)} %collective-permute-done.26.refs_6_), channel_id=1, source_target_pairs={{0,4},{4,0},{8,12},{12,8},{16,20},{20,16},{24,28},{28,24},{1,5},{5... | collective-permute-start | bytes 1769480 | tf_op jit(solution)/shard_map/ppermute | solution.py:102
  263.3 52.9 %collective-permute-start.35 = (bf16[2,3,96,512]{3,2,1,0:T(8,128)(2,1)}, bf16[2,3,96,512]{3,2,1,0:T(8,128)(2,1)}, u32[]{:S(2)}, u32[]{:S(2)}) collective-permute-start(bf16[2,3,96,512]{3,2,1,0:T(8,128)(2,1)} %get-tuple-element.206.refs_0_), channel_id=1, source_target_pairs={{0,4},{4,0},{8,12},{12,8},{16,20},{20,16},{24,28},{28,24},{1,5},{5... | collective-permute-start | bytes 1769480 | tf_op jit(solution)/shard_map/ppermute | solution.py:102
  265.7 51.0 %collective-permute-start.43 = (bf16[2,3,96,512]{3,2,1,0:T(8,128)(2,1)S(1)}, bf16[2,3,96,512]{3,2,1,0:T(8,128)(2,1)}, u32[]{:S(2)}, u32[]{:S(2)}) collective-permute-start(bf16[2,3,96,512]{3,2,1,0:T(8,128)(2,1)S(1)} %copy-done.53), channel_id=1, source_target_pairs={{0,8},{4,12},{8,0},{12,4},{16,24},{20,28},{24,16},{28,20},{1,9},{5... | collective-permute-start | bytes 1769480 | tf_op jit(solution)/shard_map/ppermute | solution.py:102
  276.3 41.8 %collective-permute-start.30 = (bf16[2,3,96,512]{3,2,1,0:T(8,128)(2,1)}, bf16[2,3,96,512]{3,2,1,0:T(8,128)(2,1)}, u32[]{:S(2)}, u32[]{:S(2)}) collective-permute-start(bf16[2,3,96,512]{3,2,1,0:T(8,128)(2,1)} %collective-permute-done.29.refs_2_), channel_id=1, source_target_pairs={{0,4},{4,0},{8,12},{12,8},{16,20},{20,16},{24,28},{28,24},{1,5},{5... | collective-permute-start | bytes 1769480 | tf_op jit(solution)/shard_map/ppermute | solution.py:102
  277.8 41.4 %collective-permute-start.32 = (bf16[2,3,96,512]{3,2,1,0:T(8,128)(2,1)}, bf16[2,3,96,512]{3,2,1,0:T(8,128)(2,1)}, u32[]{:S(2)}, u32[]{:S(2)}) collective-permute-start(bf16[2,3,96,512]{3,2,1,0:T(8,128)(2,1)} %collective-permute-done.31.refs_4_), channel_id=1, source_target_pairs={{0,4},{4,0},{8,12},{12,8},{16,20},{20,16},{24,28},{28,24},{1,5},{5... | collective-permute-start | bytes 1769480 | tf_op jit(solution)/shard_map/ppermute | solution.py:102
  278.4 41.8 %collective-permute-start.34 = (bf16[2,3,96,512]{3,2,1,0:T(8,128)(2,1)}, bf16[2,3,96,512]{3,2,1,0:T(8,128)(2,1)}, u32[]{:S(2)}, u32[]{:S(2)}) collective-permute-start(bf16[2,3,96,512]{3,2,1,0:T(8,128)(2,1)} %collective-permute-done.33.refs_6_), channel_id=1, source_target_pairs={{0,4},{4,0},{8,12},{12,8},{16,20},{20,16},{24,28},{28,24},{1,5},{5... | collective-permute-start | bytes 1769480 | tf_op jit(solution)/shard_map/ppermute | solution.py:102
  316.7 39.6 %collective-permute-start.47 = (bf16[2,3,96,512]{3,2,1,0:T(8,128)(2,1)S(1)}, bf16[2,3,96,512]{3,2,1,0:T(8,128)(2,1)}, u32[]{:S(2)}, u32[]{:S(2)}) collective-permute-start(bf16[2,3,96,512]{3,2,1,0:T(8,128)(2,1)S(1)} %copy-done.53), channel_id=1, source_target_pairs={{0,24},{4,28},{8,16},{12,20},{16,8},{20,12},{24,0},{28,4},{1,25},{... | collective-permute-start | bytes 1769480 | tf_op jit(solution)/shard_map/ppermute | solution.py:102
  319.3 39.1 %collective-permute-start.39 = (bf16[2,3,96,512]{3,2,1,0:T(8,128)(2,1)}, bf16[2,3,96,512]{3,2,1,0:T(8,128)(2,1)}, u32[]{:S(2)}, u32[]{:S(2)}) collective-permute-start(bf16[2,3,96,512]{3,2,1,0:T(8,128)(2,1)} %copy-done.72), channel_id=1, source_target_pairs={{0,4},{4,0},{8,12},{12,8},{16,20},{20,16},{24,28},{28,24},{1,5},{5... | collective-permute-start | bytes 1769480 | tf_op jit(solution)/shard_map/ppermute | solution.py:102
  354.7 42.2 %collective-permute-start.42 = (bf16[2,3,96,512]{3,2,1,0:T(8,128)(2,1)S(1)}, bf16[2,3,96,512]{3,2,1,0:T(8,128)(2,1)}, u32[]{:S(2)}, u32[]{:S(2)}) collective-permute-start(bf16[2,3,96,512]{3,2,1,0:T(8,128)(2,1)S(1)} %copy-done.53), channel_id=1, source_target_pairs={{0,4},{4,0},{8,12},{12,8},{16,20},{20,16},{24,28},{28,24},{1,5},{5... | collective-permute-start | bytes 1769480 | tf_op jit(solution)/shard_map/ppermute | solution.py:102
  356.3 40.6 %collective-permute-start.44 = (bf16[2,3,96,512]{3,2,1,0:T(8,128)(2,1)}, bf16[2,3,96,512]{3,2,1,0:T(8,128)(2,1)}, u32[]{:S(2)}, u32[]{:S(2)}) collective-permute-start(bf16[2,3,96,512]{3,2,1,0:T(8,128)(2,1)} %collective-permute-done.43.refs_2_), channel_id=1, source_target_pairs={{0,4},{4,0},{8,12},{12,8},{16,20},{20,16},{24,28},{28,24},{1,5},{5... | collective-permute-start | bytes 1769480 | tf_op jit(solution)/shard_map/ppermute | solution.py:102
  356.7 40.2 %collective-permute-start.46 = (bf16[2,3,96,512]{3,2,1,0:T(8,128)(2,1)}, bf16[2,3,96,512]{3,2,1,0:T(8,128)(2,1)}, u32[]{:S(2)}, u32[]{:S(2)}) collective-permute-start(bf16[2,3,96,512]{3,2,1,0:T(8,128)(2,1)} %collective-permute-done.45.refs_4_), channel_id=1, source_target_pairs={{0,4},{4,0},{8,12},{12,8},{16,20},{20,16},{24,28},{28,24},{1,5},{5... | collective-permute-start | bytes 1769480 | tf_op jit(solution)/shard_map/ppermute | solution.py:102
  358.3 50.6 %collective-permute-start.48 = (bf16[2,3,96,512]{3,2,1,0:T(8,128)(2,1)}, bf16[2,3,96,512]{3,2,1,0:T(8,128)(2,1)}, u32[]{:S(2)}, u32[]{:S(2)}) collective-permute-start(bf16[2,3,96,512]{3,2,1,0:T(8,128)(2,1)} %collective-permute-done.47.refs_6_), channel_id=1, source_target_pairs={{0,4},{4,0},{8,12},{12,8},{16,20},{20,16},{24,28},{28,24},{1,5},{5... | collective-permute-start | bytes 1769480 | tf_op jit(solution)/shard_map/ppermute | solution.py:102
  358.8 121.1 %collective-permute-start.72 = (bf16[4,2,3,96,512]{4,3,2,1,0:T(8,128)(2,1)}, bf16[4,2,3,96,512]{4,3,2,1,0:T(8,128)(2,1)}, u32[]{:S(2)}, u32[]{:S(2)}) collective-permute-start(bf16[4,2,3,96,512]{4,3,2,1,0:T(8,128)(2,1)} %get-tuple-element.66), channel_id=1, source_target_pairs={{0,4},{4,0},{8,12},{12,8},{16,20},{20,16},{24,28},{28,24},{1,5},{5... | collective-permute-start | bytes 7077896 | tf_op jit(solution)/shard_map/ppermute | solution.py:102
  465.4 59.3 %collective-permute-start.76 = (bf16[4,2,3,96,512]{4,3,2,1,0:T(8,128)(2,1)}, bf16[4,2,3,96,512]{4,3,2,1,0:T(8,128)(2,1)}, u32[]{:S(2)}, u32[]{:S(2)}) collective-permute-start(bf16[4,2,3,96,512]{4,3,2,1,0:T(8,128)(2,1)} %get-tuple-element.68), channel_id=1, source_target_pairs={{0,4},{4,0},{8,12},{12,8},{16,20},{20,16},{24,28},{28,24},{1,5},{5... | collective-permute-start | bytes 7077896 | tf_op jit(solution)/shard_map/ppermute | solution.py:102
  467.0 103.3 %collective-permute-start.80 = (bf16[4,2,3,96,512]{4,3,2,1,0:T(8,128)(2,1)}, bf16[4,2,3,96,512]{4,3,2,1,0:T(8,128)(2,1)}, u32[]{:S(2)}, u32[]{:S(2)}) collective-permute-start(bf16[4,2,3,96,512]{4,3,2,1,0:T(8,128)(2,1)} %get-tuple-element.70), channel_id=1, source_target_pairs={{0,4},{4,0},{8,12},{12,8},{16,20},{20,16},{24,28},{28,24},{1,5},{5... | collective-permute-start | bytes 7077896 | tf_op jit(solution)/shard_map/ppermute | solution.py:102
  468.7 151.8 %collective-permute-start.84 = (bf16[4,2,3,96,512]{4,3,2,1,0:T(8,128)(2,1)}, bf16[4,2,3,96,512]{4,3,2,1,0:T(8,128)(2,1)}, u32[]{:S(2)}, u32[]{:S(2)}) collective-permute-start(bf16[4,2,3,96,512]{4,3,2,1,0:T(8,128)(2,1)} %get-tuple-element.72), channel_id=1, source_target_pairs={{0,4},{4,0},{8,12},{12,8},{16,20},{20,16},{24,28},{28,24},{1,5},{5... | collective-permute-start | bytes 7077896 | tf_op jit(solution)/shard_map/ppermute | solution.py:102
  479.9 40.5 %collective-permute-start.52 = (bf16[512,768]{1,0:T(8,128)(2,1)}, bf16[512,768]{1,0:T(8,128)(2,1)}, u32[]{:S(2)}, u32[]{:S(2)}) collective-permute-start(bf16[512,768]{1,0:T(8,128)(2,1)} %fusion.32), channel_id=1, source_target_pairs={{0,2},{1,3},{2,0},{3,1},{4,6},{5,7},{6,4},{7,5},{8,10},{9,11},{10,... | collective-permute-start | bytes 2359304 | tf_op jit(solution)/shard_map/ppermute | solution.py:102
  499.8 137.2 %collective-permute-start.73 = (bf16[2,3,96,512]{3,2,1,0:T(8,128)(2,1)}, bf16[2,3,96,512]{3,2,1,0:T(8,128)(2,1)}, u32[]{:S(2)}, u32[]{:S(2)}) collective-permute-start(bf16[2,3,96,512]{3,2,1,0:T(8,128)(2,1)} %get-tuple-element.191), channel_id=1, source_target_pairs={{0,8},{4,12},{8,0},{12,4},{16,24},{20,28},{24,16},{28,20},{1,9},{5... | collective-permute-start | bytes 1769480 | tf_op jit(solution)/shard_map/ppermute | solution.py:102
  520.5 118.5 %collective-permute-start.74 = (bf16[2,3,96,512]{3,2,1,0:T(8,128)(2,1)}, bf16[2,3,96,512]{3,2,1,0:T(8,128)(2,1)}, u32[]{:S(2)}, u32[]{:S(2)}) collective-permute-start(bf16[2,3,96,512]{3,2,1,0:T(8,128)(2,1)} %get-tuple-element.193), channel_id=1, source_target_pairs={{0,16},{4,20},{8,24},{12,28},{16,0},{20,4},{24,8},{28,12},{1,17},{... | collective-permute-start | bytes 1769480 | tf_op jit(solution)/shard_map/ppermute | solution.py:102
  524.7 123.1 %collective-permute-start.75 = (bf16[2,3,96,512]{3,2,1,0:T(8,128)(2,1)}, bf16[2,3,96,512]{3,2,1,0:T(8,128)(2,1)}, u32[]{:S(2)}, u32[]{:S(2)}) collective-permute-start(bf16[2,3,96,512]{3,2,1,0:T(8,128)(2,1)} %get-tuple-element.192), channel_id=1, source_target_pairs={{0,24},{4,28},{8,16},{12,20},{16,8},{20,12},{24,0},{28,4},{1,25},{... | collective-permute-start | bytes 1769480 | tf_op jit(solution)/shard_map/ppermute | solution.py:102
  579.8 68.0 %collective-permute-start.77 = (bf16[2,3,96,512]{3,2,1,0:T(8,128)(2,1)}, bf16[2,3,96,512]{3,2,1,0:T(8,128)(2,1)}, u32[]{:S(2)}, u32[]{:S(2)}) collective-permute-start(bf16[2,3,96,512]{3,2,1,0:T(8,128)(2,1)} %get-tuple-element.194), channel_id=1, source_target_pairs={{0,8},{4,12},{8,0},{12,4},{16,24},{20,28},{24,16},{28,20},{1,9},{5... | collective-permute-start | bytes 1769480 | tf_op jit(solution)/shard_map/ppermute | solution.py:102
  647.8 82.1 %collective-permute-start.53 = (bf16[512,768]{1,0:T(8,128)(2,1)}, bf16[512,768]{1,0:T(8,128)(2,1)S(1)}, u32[]{:S(2)}, u32[]{:S(2)}) collective-permute-start(bf16[512,768]{1,0:T(8,128)(2,1)} %fusion.91), channel_id=1, source_target_pairs={{0,1},{1,0},{2,3},{3,2},{4,5},{5,4},{6,7},{7,6},{8,9},{9,8},{10,11... | collective-permute-start | bytes 2359304 | tf_op jit(solution)/shard_map/ppermute | solution.py:102
  647.8 39.7 %collective-permute-start.81 = (bf16[2,3,96,512]{3,2,1,0:T(8,128)(2,1)}, bf16[2,3,96,512]{3,2,1,0:T(8,128)(2,1)S(1)}, u32[]{:S(2)}, u32[]{:S(2)}) collective-permute-start(bf16[2,3,96,512]{3,2,1,0:T(8,128)(2,1)} %get-tuple-element.197), channel_id=1, source_target_pairs={{0,8},{4,12},{8,0},{12,4},{16,24},{20,28},{24,16},{28,20},{1,9},{5... | collective-permute-start | bytes 1769480 | tf_op jit(solution)/shard_map/ppermute | solution.py:102
  675.4 50.5 %collective-permute-start.82 = (bf16[2,3,96,512]{3,2,1,0:T(8,128)(2,1)}, bf16[2,3,96,512]{3,2,1,0:T(8,128)(2,1)S(1)}, u32[]{:S(2)}, u32[]{:S(2)}) collective-permute-start(bf16[2,3,96,512]{3,2,1,0:T(8,128)(2,1)} %get-tuple-element.199), channel_id=1, source_target_pairs={{0,16},{4,20},{8,24},{12,28},{16,0},{20,4},{24,8},{28,12},{1,17},{... | collective-permute-start | bytes 1769480 | tf_op jit(solution)/shard_map/ppermute | solution.py:102
  675.4 50.5 %collective-permute-start.83 = (bf16[2,3,96,512]{3,2,1,0:T(8,128)(2,1)}, bf16[2,3,96,512]{3,2,1,0:T(8,128)(2,1)S(1)}, u32[]{:S(2)}, u32[]{:S(2)}) collective-permute-start(bf16[2,3,96,512]{3,2,1,0:T(8,128)(2,1)} %get-tuple-element.198), channel_id=1, source_target_pairs={{0,24},{4,28},{8,16},{12,20},{16,8},{20,12},{24,0},{28,4},{1,25},{... | collective-permute-start | bytes 1769480 | tf_op jit(solution)/shard_map/ppermute | solution.py:102
  677.8 52.2 %collective-permute-start.55 = (bf16[512,768]{1,0:T(8,128)(2,1)}, bf16[512,768]{1,0:T(8,128)(2,1)S(1)}, u32[]{:S(2)}, u32[]{:S(2)}) collective-permute-start(bf16[512,768]{1,0:T(8,128)(2,1)} %collective-permute-done.54), channel_id=1, source_target_pairs={{0,1},{1,0},{2,3},{3,2},{4,5},{5,4},{6,7},{7,6},{8,9},{9,8},{10,11... | collective-permute-start | bytes 2359304 | tf_op jit(solution)/shard_map/ppermute | solution.py:102
  687.4 116.5 %collective-permute-start.85 = (bf16[2,3,96,512]{3,2,1,0:T(8,128)(2,1)}, bf16[2,3,96,512]{3,2,1,0:T(8,128)(2,1)}, u32[]{:S(2)}, u32[]{:S(2)}) collective-permute-start(bf16[2,3,96,512]{3,2,1,0:T(8,128)(2,1)} %get-tuple-element.200), channel_id=1, source_target_pairs={{0,8},{4,12},{8,0},{12,4},{16,24},{20,28},{24,16},{28,20},{1,9},{5... | collective-permute-start | bytes 1769480 | tf_op jit(solution)/shard_map/ppermute | solution.py:102
  725.9 78.1 %collective-permute-start.86 = (bf16[2,3,96,512]{3,2,1,0:T(8,128)(2,1)}, bf16[2,3,96,512]{3,2,1,0:T(8,128)(2,1)}, u32[]{:S(2)}, u32[]{:S(2)}) collective-permute-start(bf16[2,3,96,512]{3,2,1,0:T(8,128)(2,1)} %get-tuple-element.202), channel_id=1, source_target_pairs={{0,16},{4,20},{8,24},{12,28},{16,0},{20,4},{24,8},{28,12},{1,17},{... | collective-permute-start | bytes 1769480 | tf_op jit(solution)/shard_map/ppermute | solution.py:102
  725.9 78.1 %collective-permute-start.87 = (bf16[2,3,96,512]{3,2,1,0:T(8,128)(2,1)}, bf16[2,3,96,512]{3,2,1,0:T(8,128)(2,1)}, u32[]{:S(2)}, u32[]{:S(2)}) collective-permute-start(bf16[2,3,96,512]{3,2,1,0:T(8,128)(2,1)} %get-tuple-element.201), channel_id=1, source_target_pairs={{0,24},{4,28},{8,16},{12,20},{16,8},{20,12},{24,0},{28,4},{1,25},{... | collective-permute-start | bytes 1769480 | tf_op jit(solution)/shard_map/ppermute | solution.py:102
  807.4 54.5 %collective-permute-start.57 = (bf16[512,768]{1,0:T(8,128)(2,1)}, bf16[512,768]{1,0:T(8,128)(2,1)}, u32[]{:S(2)}, u32[]{:S(2)}) collective-permute-start(bf16[512,768]{1,0:T(8,128)(2,1)} %fusion.30), channel_id=1, source_target_pairs={{0,2},{1,3},{2,0},{3,1},{4,6},{5,7},{6,4},{7,5},{8,10},{9,11},{10,... | collective-permute-start | bytes 2359304 | tf_op jit(solution)/shard_map/ppermute | solution.py:102
  821.8 43.5 %collective-permute-start.64 = (bf16[96,1024]{1,0:T(8,128)(2,1)S(1)}, bf16[96,1024]{1,0:T(8,128)(2,1)S(1)}, u32[]{:S(2)}, u32[]{:S(2)}) collective-permute-start(bf16[96,1024]{1,0:T(8,128)(2,1)S(1)} %get-tuple-element.218), channel_id=1, source_target_pairs={{0,8},{4,12},{8,0},{12,4},{16,24},{20,28},{24,16},{28,20},{1,9},{5... | collective-permute-start | bytes 589832 | tf_op jit(solution)/shard_map/ppermute | solution.py:102
  (115 other events, 1556.3 us)
Sparse Core Ops, SparseCore 0:
  468.8 28.2 reduce-scatter.1

commit v2 on v1

--- a/solution.py
+++ b/solution.py
@@ -14,7 +14,7 @@
 PAD = 256
 BLOCK = 256
 TILE = 256
-GROUPS = 4
+GROUPS = 2
 
 epsilon = 1e-06
 HIGHEST = lax.Precision.HIGHEST
@@ -129,22 +129,49 @@
     return mine + swap(other.astype(BF16), "tensor", 2).astype(F32)
 
 
-def pieces_of(own, axis):
-    if lax.axis_size("dp") != 8:
-        return [lax.all_gather(own, "dp", axis=axis, tiled=True)]
-    column = [own, swap(own, "dp", 2), swap(own, "dp", 4), swap(own, "dp", 6)]
-    pieces = []
-    for shard in column:
-        pieces += [shard, swap(shard, "dp", 1)]
-    return pieces
-
-
-def sum_pieces(mine, theirs):
-    paired = mine.astype(F32) + swap(theirs, "dp", 1).astype(F32)
-    total = paired[0]
-    for j in range(1, 4):
-        total = total + swap(paired[j].astype(BF16), "dp", 2 * j).astype(F32)
-    return total
+def together(*values):
+    return lax.optimization_barrier(values)
+
+
+def column_groups():
+    size = lax.axis_size("dp")
+    return [list(range(first, size, 2)) for first in range(2)]
+
+
+def gather_column(own):
+    return lax.all_gather(own, "dp", axis=0, tiled=False, axis_index_groups=column_groups())
+
+
+def scatter_column(parts):
+    return lax.psum_scatter(
+        parts, "dp", scatter_dimension=0, tiled=False, axis_index_groups=column_groups()
+    )
+
+
+def by_parity(mine, other):
+    even = lax.axis_index("dp") % 2 == 0
+    return jnp.stack([jnp.where(even, mine, other), jnp.where(even, other, mine)])
+
+
+def gather_pair(own):
+    half = own.shape[0] // 2
+    far, across = swap(own, "tensor", 2), swap(own, "dp", 1)
+    corner = jnp.concatenate(
+        [swap(across[:half], "tensor", 2), swap(far[half:], "dp", 1)], axis=0
+    )
+    near = [swap(piece, "tensor", 1) for piece in (own, far, across, corner)]
+    return [own, near[0], far, near[1], across, near[2], corner, near[3]]
+
+
+def scatter_pair(keep, send):
+    half = keep.shape[1] // 2
+    keep = keep.astype(F32) + swap(send, "tensor", 1).astype(F32)
+    mine, far, across, corner = keep[0], keep[1], keep[2], keep[3].astype(BF16)
+    from_far = swap(corner[:half], "tensor", 2).astype(F32)
+    from_across = swap(corner[half:], "dp", 1).astype(F32)
+    far = jnp.concatenate([far[:half], far[half:] + from_across], axis=0).astype(BF16)
+    across = jnp.concatenate([across[:half] + from_far, across[half:]], axis=0).astype(BF16)
+    return mine + swap(far, "tensor", 2).astype(F32) + swap(across, "dp", 1).astype(F32)
 
 
 def sum_all(values):
@@ -400,130 +427,147 @@
     )(queries, grads, out, keys, values, keys_t, rowinfo, colinfo, totals, cos_table, sin_table)
 
 
-def experts_kernel(
-    first, n_in, n_out, counts_ref, place_ref, rows_ref, grads_ref, slot_row_ref, gate_row_ref,
-    slot_col_ref, gate_col_ref, *refs
-):
-    in_refs, refs = refs[:n_in], refs[n_in:]
-    sum_ref, grad_in_ref, gate_grad_ref = refs[:3]
-    out_refs, refs = refs[3 : 3 + n_out], refs[3 + n_out :]
-    weight, grad_weight, sum_acc, grad_in_acc = refs
+def experts_kernel(whole_weights, base_ref, counts_ref, slot_rows_ref, slot_cols_ref, weights_ref, *refs):
+    rows_refs, grads_refs, refs = refs[:8], refs[8:16], refs[16:]
+    sum_refs, grad_in_refs, out_ref, weight, grad_weight, gates = (
+        refs[0:2], refs[2:4], refs[4], refs[5], refs[6], refs[7],
+    )
     step = pl.program_id(0)
-    expert = first + step
-    tokens, width = rows_ref.shape
-    hidden = weight.shape[2]
-    span = 512
+    expert = base_ref[0] + step
+    rows, width = grads_refs[0].shape
 
     @pl.when(step == 0)
     def _():
-        sum_acc[...] = jnp.zeros_like(sum_acc)
-        grad_in_acc[...] = jnp.zeros_like(grad_in_acc)
-        gate_grad_ref[...] = jnp.zeros_like(gate_grad_ref)
+        for ref in (*sum_refs, *grad_in_refs):
+            ref[...] = jnp.zeros_like(ref)
+        for k in range(8):
+            at = pl.ds((k % 4) * rows, rows)
+            gates[k // 4, :, at] = rows_refs[k][:, width:].astype(F32).T
 
     grad_weight[...] = jnp.zeros_like(grad_weight)
-    if n_in == 1:
-        weight[...] = in_refs[0][0]
+    if whole_weights:
+        weight[...] = weights_ref[0]
     else:
-        share = width // n_in
-        for k in range(n_in):
-            at = pl.ds(pl.multiple_of(place_ref[k] * share, share), share)
-            weight[:, at, :] = in_refs[k][0]
-
-    lane = lax.broadcasted_iota(jnp.int32, slot_col_ref.shape, 1)
-    slot_col = jnp.sum(jnp.where(lane == expert, slot_col_ref[...], 0), axis=1, keepdims=True)
-    gate_col = jnp.sum(jnp.where(lane == expert, gate_col_ref[...], 0.0), axis=1, keepdims=True)
-    slot_row, gate_row = slot_row_ref[0], gate_row_ref[0]
-
-    def tile(c, carry):
-        down = c * TILE + lax.broadcasted_iota(jnp.int32, (TILE, 1), 0)
-        across = c * TILE + lax.broadcasted_iota(jnp.int32, (1, TILE), 1)
-        picked = slot_row == down
-        inputs = dot_nn(jnp.where(picked, 1.0, 0.0).astype(BF16), rows_ref[...]).astype(BF16)
-        grad_out = dot_nn(jnp.where(picked, gate_row, 0.0).astype(BF16), grads_ref[...]).astype(BF16)
-        gate_part = dot_nn(inputs, weight[0])
-        up_part = dot_nn(inputs, weight[1])
-        sigmoid = 1.0 / (1.0 + jnp.exp(-gate_part))
-        swish = gate_part * sigmoid
-        act = (swish * up_part).astype(BF16)
-        expert_out = dot_nt(act, weight[2]).astype(BF16)
-        grad_act = dot_nn(grad_out, weight[2])
-        grad_gate = (grad_act * up_part * sigmoid * (1.0 + gate_part * (1.0 - sigmoid))).astype(BF16)
-        grad_up = (grad_act * swish).astype(BF16)
-        grad_weight[0] += dot_tn(inputs, grad_gate)
-        grad_weight[1] += dot_tn(inputs, grad_up)
-        grad_weight[2] += dot_tn(grad_out, act)
-        grad_in = (dot_nt(grad_gate, weight[0]) + dot_nt(grad_up, weight[1])).astype(BF16)
-        for b in range(tokens // span):
-            at = pl.ds(b * span, span)
-            back = jnp.where(slot_col[b * span : (b + 1) * span] == across, 1.0, 0.0).astype(BF16)
-            part = dot_nn(back, expert_out)
-            sum_acc[at, :] += gate_col[b * span : (b + 1) * span] * part
-            along = jnp.sum(part * grads_ref[at, :].astype(F32), axis=1, keepdims=True)
-            lanes = lax.broadcasted_iota(jnp.int32, (span, gate_grad_ref.shape[1]), 1)
-            gate_grad_ref[at, :] += jnp.where(lanes == expert, along, 0.0)
-            grad_in_acc[at, :] += dot_nn(back, grad_in)
-        return carry
-
-    lax.fori_loop(0, (counts_ref[expert] + TILE - 1) // TILE, tile, 0)
-
-    if n_out == 1:
-        out_refs[0][0] = grad_weight[...].astype(BF16)
+        depth, _, _, _, share, _ = weights_ref.shape
+        for z in range(depth):
+            for y in range(2):
+                weight[:, pl.ds((2 * z + y) * share, share), :] = weights_ref[z, y, 0]
+
+    def tree(a):
+        slot_row = slot_rows_ref[a, pl.ds(expert, 1), :]
+        gate_row = gates[a, pl.ds(expert, 1), :]
+
+        def tile(c, carry):
+            down = c * TILE + lax.broadcasted_iota(jnp.int32, (TILE, 1), 0)
+            across = c * TILE + lax.broadcasted_iota(jnp.int32, (1, TILE), 1)
+            inputs = jnp.zeros((TILE, width), F32)
+            grad_out = jnp.zeros((TILE, width), F32)
+            for b in range(4):
+                picked = slot_row[:, b * rows : (b + 1) * rows] == down
+                gate = gate_row[:, b * rows : (b + 1) * rows]
+                inputs = inputs + dot_nn(
+                    jnp.where(picked, 1.0, 0.0).astype(BF16), rows_refs[4 * a + b][:, :width]
+                )
+                grad_out = grad_out + dot_nn(
+                    jnp.where(picked, gate, 0.0).astype(BF16), grads_refs[4 * a + b][...]
+                )
+            inputs, grad_out = inputs.astype(BF16), grad_out.astype(BF16)
+            gate_part = dot_nn(inputs, weight[0])
+            up_part = dot_nn(inputs, weight[1])
+            sigmoid = 1.0 / (1.0 + jnp.exp(-gate_part))
+            swish = gate_part * sigmoid
+            act = (swish * up_part).astype(BF16)
+            expert_out = dot_nt(act, weight[2]).astype(BF16)
+            grad_act = dot_nn(grad_out, weight[2])
+            grad_gate = (
+                grad_act * up_part * sigmoid * (1.0 + gate_part * (1.0 - sigmoid))
+            ).astype(BF16)
+            grad_up = (grad_act * swish).astype(BF16)
+            grad_weight[0] += dot_tn(inputs, grad_gate)
+            grad_weight[1] += dot_tn(inputs, grad_up)
+            grad_weight[2] += dot_tn(grad_out, act)
+            grad_in = (dot_nt(grad_gate, weight[0]) + dot_nt(grad_up, weight[1])).astype(BF16)
+            for b in range(4):
+                k = 4 * a + b
+                lane = lax.broadcasted_iota(jnp.int32, (rows, 8), 1)
+                slot_col = jnp.sum(
+                    jnp.where(lane == expert, slot_cols_ref[pl.ds(k * rows, rows), :], 0),
+                    axis=1,
+                    keepdims=True,
+                )
+                lane = lax.broadcasted_iota(jnp.int32, (rows, 128), 1)
+                gate_col = jnp.sum(
+                    jnp.where(lane == expert, rows_refs[k][:, width:].astype(F32), 0.0),
+                    axis=1,
+                    keepdims=True,
+                )
+                back = jnp.where(slot_col == across, 1.0, 0.0).astype(BF16)
+                part = dot_nn(back, expert_out)
+                sum_ref, grad_in_ref = sum_refs[b % 2], grad_in_refs[b % 2]
+                at = 2 * a + b // 2
+                sum_ref[at] = (sum_ref[at].astype(F32) + gate_col * part).astype(BF16)
+                along = jnp.sum(part * grads_refs[k][...].astype(F32), axis=1, keepdims=True)
+                grad_in_ref[at, :, :width] = (
+                    grad_in_ref[at, :, :width].astype(F32) + dot_nn(back, grad_in)
+                ).astype(BF16)
+                grad_in_ref[at, :, width:] = (
+                    grad_in_ref[at, :, width:].astype(F32) + jnp.where(lane == expert, along, 0.0)
+                ).astype(BF16)
+            return carry
+
+        lax.fori_loop(0, (counts_ref[a, expert] + TILE - 1) // TILE, tile, 0)
+
+    tree(0)
+    tree(1)
+    if whole_weights:
+        out_ref[0] = grad_weight[...].astype(BF16)
     else:
-        for j in range(n_in // 2):
-            for which in range(2):
-                at = pl.ds(pl.multiple_of(place_ref[2 * j + which] * share, share), share)
-                out_refs[which][j, 0] = grad_weight[:, at, :].astype(BF16)
-
-    @pl.when(step == pl.num_programs(0) - 1)
-    def _():
-        sum_ref[...] = sum_acc[...].astype(BF16)
-        grad_in_ref[...] = grad_in_acc[...].astype(BF16)
-
-
-def experts(first, pieces, counts, place, rows, grads, slot_rows, gate_rows, slot_cols, gate_cols):
-    tokens, width = rows.shape
-    group, kinds, share, hidden = pieces[0].shape
-    n_in = len(pieces)
+        for z in range(depth):
+            for y in range(2):
+                at = pl.ds((2 * z + y) * share, share)
+                out_ref[z, y, 0] = grad_weight[:, at, :].astype(BF16)
+
+
+def experts(base, weights, counts, rows, grads, slot_rows, slot_cols):
+    count, width = grads[0].shape
+    wide = rows[0].shape[1]
+    whole_weights = weights.ndim == 4
+    kinds, share, hidden = weights.shape[-3:]
+    group = weights.shape[0] if whole_weights else weights.shape[2]
+    depth = width if whole_weights else 2 * weights.shape[0] * share
     whole = lambda a: pl.BlockSpec(a.shape, lambda e, *_: (0,) * a.ndim, pipeline_mode=pl.Buffered(1))
-    by_expert = pl.BlockSpec((1, 1, tokens), lambda e, *_: (first + e, 0, 0))
-    piece_spec = pl.BlockSpec((1, kinds, share, hidden), lambda e, *_: (e, 0, 0, 0))
-    token_spec = lambda w: pl.BlockSpec((tokens, w), lambda e, *_: (0, 0), pipeline_mode=pl.Buffered(1))
-    if n_in == 1:
-        grad_specs = [piece_spec]
-        grad_shapes = [jax.ShapeDtypeStruct(pieces[0].shape, BF16)]
+    if whole_weights:
+        weight_spec = pl.BlockSpec((1, kinds, share, hidden), lambda e, *_: (e, 0, 0, 0))
     else:
-        half = n_in // 2
-        grad_specs = [pl.BlockSpec((half, 1, kinds, share, hidden), lambda e, *_: (0, e, 0, 0, 0))] * 2
-        grad_shapes = [jax.ShapeDtypeStruct((half, group, kinds, share, hidden), BF16)] * 2
-    slots = tokens // 4
+        weight_spec = pl.BlockSpec(
+            (weights.shape[0], 2, 1, kinds, share, hidden), lambda e, *_: (0, 0, e, 0, 0, 0)
+        )
+    sums = jax.ShapeDtypeStruct((4, count, width), BF16)
+    grad_ins = jax.ShapeDtypeStruct((4, count, wide), BF16)
+    slots = count * 2
     return pl.pallas_call(
-        functools.partial(experts_kernel, first, n_in, len(grad_specs)),
+        functools.partial(experts_kernel, whole_weights),
         grid_spec=pltpu.PrefetchScalarGridSpec(
             num_scalar_prefetch=2,
             grid=(group,),
-            in_specs=[whole(rows), whole(grads), by_expert, by_expert, whole(slot_cols), whole(gate_cols)]
-            + [piece_spec] * n_in,
-            out_specs=[token_spec(width), token_spec(width), token_spec(128)] + grad_specs,
+            in_specs=[whole(slot_rows), whole(slot_cols), weight_spec]
+            + [whole(a) for a in rows]
+            + [whole(a) for a in grads],
+            out_specs=[whole(sums), whole(sums), whole(grad_ins), whole(grad_ins), weight_spec],
             scratch_shapes=[
-                pltpu.VMEM((kinds, width, hidden), BF16),
-                pltpu.VMEM((kinds, width, hidden), F32),
-                pltpu.VMEM((tokens, width), F32),
-                pltpu.VMEM((tokens, width), F32),
+                pltpu.VMEM((kinds, depth, hidden), BF16),
+                pltpu.VMEM((kinds, depth, hidden), F32),
+                pltpu.VMEM((2, wide - width, 4 * count), F32),
             ],
         ),
-        out_shape=[
-            jax.ShapeDtypeStruct((tokens, width), BF16),
-            jax.ShapeDtypeStruct((tokens, width), BF16),
-            jax.ShapeDtypeStruct((tokens, 128), F32),
-        ]
-        + grad_shapes,
+        out_shape=[sums, sums, grad_ins, grad_ins, jax.ShapeDtypeStruct(weights.shape, BF16)],
         compiler_params=pltpu.CompilerParams(vmem_limit_bytes=60 << 20),
         cost_estimate=pl.CostEstimate(
-            flops=group * slots * width * (18 * hidden + 8 * tokens),
-            bytes_accessed=16 * tokens * width,
+            flops=group * slots * width * (18 * hidden + 32 * count),
+            bytes_accessed=64 * count * width,
             transcendentals=0,
         ),
-    )(counts, place, rows, grads, slot_rows, gate_rows, slot_cols, gate_cols, *pieces)
+    )(base, counts, slot_rows, slot_cols, weights, *rows, *grads)
 
 
 def per_device(
@@ -549,9 +593,11 @@
     head_width = head_weight.shape[2]
     heads = head_width // HEAD
     share = head_weight.shape[1]
-    group = NF // GROUPS
-    me = lax.axis_index("dp")
-    place = me ^ jnp.arange(8, dtype=jnp.int32)
+    parity = lax.axis_index("dp") % 2
+    index = lax.axis_index("tensor")
+    own_experts = NF // 2
+    group = own_experts // GROUPS
+    layered = share % 16 == 0
 
     by_section = jnp.concatenate([head_weight, output_weight.T[None]], axis=0).astype(BF16)
     by_section = jnp.pad(by_section, ((0, 0), (0, 0), (0, PAD - head_width)))
@@ -563,24 +609,31 @@
     token_values = tokens_in.astype(F32)
     normed_one = normed(token_values, attention_gain).astype(BF16)
     gathered_one = gather_tensor(normed_one)
-    head_pieces = pieces_of(head_pack, 0)
-    if len(head_pieces) == 1:
-        head_full = head_pieces[0]
-    else:
-        stacked = jnp.zeros((len(head_pieces), share, 4 * PAD), BF16)
-        for k, piece in enumerate(head_pieces):
-            stacked = lax.dynamic_update_slice(stacked, piece[None], (place[k], 0, 0))
-        head_full = stacked.reshape(width, 4 * PAD)
-    expert_pieces = [
-        pieces_of(expert_pack[g * group : (g + 1) * group], 2) for g in range(GROUPS)
-    ]
-    gathered_grads = gather_tensor(cotangent)
-
-    hot = jnp.sum((routes[:, :, None] == jnp.arange(NF, dtype=jnp.int32)).astype(jnp.int32), axis=1)
-    rank = jnp.cumsum(hot, axis=0) - hot
-    counts = jnp.sum(hot, axis=0)
-    slot_cols = jnp.where(hot > 0, rank, -1)
-    slot_rows = slot_cols.T[:, None, :]
+    column = gather_column(head_pack)
+    head_full = jnp.moveaxis(by_parity(column, swap(column, "dp", 1)), 0, 1).reshape(width, 4 * PAD)
+    expert_weights = []
+    kept = lax.dynamic_slice_in_dim(expert_pack, parity * own_experts, own_experts, 0)
+    given = lax.dynamic_slice_in_dim(expert_pack, (1 - parity) * own_experts, own_experts, 0)
+    for g in range(GROUPS):
+        at = slice(g * group, (g + 1) * group)
+        shards = gather_column(by_parity(kept[at], swap(given[at], "dp", 1)))
+        if not layered:
+            shards = shards.transpose(2, 3, 0, 1, 4, 5).reshape(group, 3, width, -1)
+        expert_weights.append(shards)
+    grad_rows = gather_pair(cotangent)
+
+    labels = jnp.arange(NF, dtype=jnp.int32)
+    slot_cols, counts = [], []
+    for tree_routes in (routes, swap(routes, "dp", 1)):
+        hot = jnp.sum((tree_routes[:, :, None] == labels).astype(jnp.int32), axis=1)
+        rank = jnp.cumsum(hot, axis=0) - hot
+        counts.append(jnp.sum(hot, axis=0))
+        quarters = jnp.where(hot > 0, rank, -1).reshape(4, row_count, NF)
+        for b in range(4):
+            slot_cols.append(lax.dynamic_index_in_dim(quarters, index ^ b, 0, keepdims=False))
+    counts = jnp.stack(counts)
+    slot_cols = jnp.concatenate(slot_cols, axis=0)
+    slot_rows = slot_cols.reshape(2, tree_len, NF).transpose(0, 2, 1)
 
     cos_table, sin_table = rotary_tables(segment_ids, parent_ids)
     rowinfo = jnp.pad(jnp.stack([segment_ids, parent_ids]), ((0, 6), (0, 0)))
@@ -604,35 +657,27 @@
         constant_gate,
         constant_vector,
     )
-    gathered_two = gather_tensor(normed_two.astype(BF16))
-    gate_cols = gather_tensor(gates.astype(BF16)).astype(F32)
-    gate_rows = gate_cols.T[:, None, :]
-
-    sums, grad_ins, gate_grads, own_grads = [], [], [], []
+    expert_rows = gather_pair(
+        jnp.concatenate([normed_two, jnp.pad(gates, ((0, 0), (0, 128 - NF)))], axis=1).astype(BF16)
+    )
+
+    parts, own_grads = [], []
     for g in range(GROUPS):
-        part, grad_in, gate_grad, *grad_pieces = experts(
-            g * group, expert_pieces[g], counts, place, gathered_two, gathered_grads,
-            slot_rows, gate_rows, slot_cols, gate_cols,
+        base = (parity * own_experts + g * group).astype(jnp.int32).reshape(1)
+        *part, weight_grads = experts(
+            base, expert_weights[g], counts, expert_rows, grad_rows, slot_rows, slot_cols
         )
-        sums.append(part.astype(F32))
-        grad_ins.append(grad_in.astype(F32))
-        gate_grads.append(gate_grad)
-        if len(grad_pieces) == 1:
-            own_grads.append(
-                lax.psum_scatter(grad_pieces[0].astype(F32), "dp", scatter_dimension=2, tiled=True)
-            )
-        else:
-            own_grads.append(sum_pieces(*grad_pieces))
-    grad_normed_two = scatter_tensor(sum(grad_ins), row_count)
-    grad_gates = lax.psum_scatter(
-        sum(gate_grads)[:, :NF], "tensor", scatter_dimension=0, tiled=True
-    )
-    expert_total = scatter_tensor(sum(sums), row_count)
-    output = (hidden + local_sum + expert_total).astype(BF16)
-    own_grads = jnp.concatenate(own_grads, axis=0)
-    grad_first = own_grads[:, :2]
-    grad_second = own_grads[:, 2].transpose(0, 2, 1)
-
+        parts.append(part)
+        if not layered:
+            weight_grads = weight_grads.reshape(group, 3, -1, 2, share, weight_grads.shape[-1])
+            weight_grads = weight_grads.transpose(2, 3, 0, 1, 4, 5)
+        own_grads.append(scatter_column(weight_grads))
+    keep, send, grad_keep, grad_send = [
+        sum(p.astype(F32) for p in same).astype(BF16) for same in zip(*parts)
+    ]
+    both = scatter_pair(grad_keep, grad_send)
+    grad_normed_two, grad_gates = both[:, :width], both[:, width : width + NF]
+    output = (hidden + local_sum + scatter_pair(keep, send)).astype(BF16)
     grad_values_out = cotangent.astype(F32)
     (
         grad_hidden_local,
@@ -644,6 +689,7 @@
         grad_constant_vector,
     ) = pull_router((grad_normed_two, grad_gates, grad_values_out))
     grad_hidden = grad_values_out + grad_hidden_local
+    grad_hidden, own_grads[0] = together(grad_hidden, own_grads[0])
     small = [grad_expert_gain, grad_router, grad_carry, grad_constant_gate, grad_constant_vector]
     flat = sum_all(jnp.concatenate([s.reshape(-1) for s in small]))
     small_out, at = [], 0
@@ -661,24 +707,31 @@
         ),
         axis=1,
     )
+    grad_projected, own_grads[1] = together(grad_projected, own_grads[1])
+    own_grads = jnp.concatenate(own_grads, axis=1)
+    kept = lax.dynamic_index_in_dim(own_grads, parity, 0, keepdims=False)
+    given = lax.dynamic_index_in_dim(own_grads, 1 - parity, 0, keepdims=False)
+    own_grads = by_parity(kept, swap(given, "dp", 1)).reshape(NF, 3, share, -1).astype(F32)
+    grad_first = own_grads[:, :2]
+    grad_second = own_grads[:, 2].transpose(0, 2, 1)
     grad_head = dot_tn(gathered_one, grad_projected)
     grad_normed_all = dot_nt(grad_projected, head_full[:, : 3 * PAD])
     grad_normed_one = scatter_tensor(grad_normed_all, row_count)
     grad_pack = jnp.concatenate([grad_head, grad_output_t], axis=1).astype(BF16)
-    if len(head_pieces) == 1:
-        own_pack = lax.psum_scatter(grad_pack.astype(F32), "dp", scatter_dimension=0, tiled=True)
-    else:
-        blocks = grad_pack.reshape(8, share, 4 * PAD)
-        ordered = [lax.dynamic_index_in_dim(blocks, place[k], 0, keepdims=False) for k in range(8)]
-        own_pack = sum_pieces(jnp.stack(ordered[0::2]), jnp.stack(ordered[1::2]))
+    blocks = grad_pack.reshape(-1, 2, share, 4 * PAD)
+    kept = lax.dynamic_index_in_dim(blocks, parity, 1, keepdims=False)
+    given = lax.dynamic_index_in_dim(blocks, 1 - parity, 1, keepdims=False)
+    paired = kept.astype(F32) + swap(given, "dp", 1).astype(F32)
+    own_pack = scatter_column(paired.astype(BF16)).astype(F32)
     own_pack = own_pack.reshape(share, 4, PAD)[:, :, :head_width].transpose(1, 0, 2)
     grad_head_own = own_pack[:3]
     grad_output_own = own_pack[3].T
 
-    norm_values, pull_norm = jax.vjp(normed, token_values, attention_gain)
-    grad_token_part, grad_attention_gain = pull_norm(grad_normed_one)
-    grad_tokens = grad_hidden + grad_token_part
-    grad_attention_gain = sum_all(grad_attention_gain)
+    grad_attention_gain = sum_all(
+        jnp.sum(grad_head * head_full[:, : 3 * PAD].astype(F32), axis=1) / attention_gain
+    )
+    _, pull_norm = jax.vjp(lambda v: normed(v, attention_gain), token_values)
+    grad_tokens = grad_hidden + pull_norm(grad_normed_one)[0]
     return (
         output,
         grad_tokens,

time: 916 us -> 661 us (0.72)
  starting transfers between devices: 169 us -> 49.4 us
  waiting for transfers between devices: 276 us -> 159 us
  blocking collectives: 0 us -> 20.3 us
  between operations: 31.8 us -> 15.4 us
  other arithmetic: 117 us -> 101 us
  Pallas kernels: 224 us -> 213 us
    ppermute x88 -> x52, waiting for transfers between devices: 276 us -> 155 us  [swap(): return lax.ppermute(values, axis, [(i, i ^ bits) for i in range(size)])]
    ppermute x88 -> x52, starting transfers between devices: 169 us -> 48.9 us  [swap(): return lax.ppermute(values, axis, [(i, i ^ bits) for i in range(size)])]
    all_gather x0 -> x1, blocking collectives: none -> 20.3 us  [gather_column(): lax.all_gather(own, 'dp', axis=0, tiled=False, axis_index_groups=column_g...]
    add x9 -> x3, other arithmetic: 23.7 us -> 8.12 us  [the longest x1 3.09 us: per_device(): grad_tokens = grad_hidden + pull_norm(grad_normed_one)[0]]
    pallas_call x4 -> x2, Pallas kernels: 135 us -> 124 us  [experts(): pl.pallas_call(functools.partial(experts_kernel, whole_weights), grid_spe...]
    slice x2 -> x9, local copies, waits for them, and re-layouts: 0.89 us -> 10.9 us  [the longest x2 3.78 us: scatter_pair(): far[:half]]
    another operation x11 -> x18, other arithmetic: 23.7 us -> 33.4 us
    unnamed x154 -> x145, local copies, waits for them, and re-layouts: 20.9 us -> 22.8 us
  transfers between devices with their start and end apart: 89 -> 57, of which waited for: 27 -> 22; matrix products, arithmetic and copies ran while one was open for 20% -> 26% of each run, Pallas kernels for 25% -> 33%
where the time goes in v2:
time: 661 us; the launch traced here: 654 us
  Pallas kernels  213 us (32%)
  waiting for transfers between devices  159 us (24%)
  other arithmetic  101 us (15%)
  local copies, waits for them, and re-layouts  59.4 us (9%)
  starting transfers between devices  49.4 us (7%)
  matrix products  36.9 us (6%)
  blocking collectives  20.3 us (3%)
  between operations  15.4 us (2%)
    ppermute x52, waiting for transfers between devices, swap(): return lax.ppermute(values, axis, [(i, i ^ bits) for i in range(size)])  155 us
    pallas_call x2, Pallas kernels, experts(): pl.pallas_call(functools.partial(experts_kernel, whole_weights), grid_spe...  124 us
    pallas_call x1, Pallas kernels, attend_back(): pl.pallas_call(functools.partial(attend_back_kernel, heads), grid=(rows /...  53.7 us
    ppermute x52, starting transfers between devices, swap(): return lax.ppermute(values, axis, [(i, i ^ bits) for i in range(size)])  48.9 us
    pallas_call x1, Pallas kernels, attend(): pl.pallas_call(functools.partial(attend_kernel, heads), grid=(rows // BLO...  24.7 us
    another operation x11, other arithmetic  23.5 us
    unnamed x145, local copies, waits for them, and re-layouts  22.8 us
    all_gather x1, blocking collectives, gather_column(): lax.all_gather(own, 'dp', axis=0, tiled=False, axis_index_groups=column_g...  20.3 us
  transfers between devices with their start and end apart: 57, of which 22 were waited for; matrix products, arithmetic and copies ran while one was open for 26% of the time, Pallas kernels for 33%

profile of v2, /device:TPU:0, one launch (start us, length us, event | category | flops | bytes accessed | tf_op | source)
XLA Modules:
  0.0 653.8 jit_solution(12170022813196600884)
XLA Ops:
  10.9 2.9 collective-permute-start.1
  22.2 20.3 %all_gather.15 = bf16[4,96,1024]{2,1,0:T(8,128)(2,1)} all-gather(bf16[1,96,1024]{2,1,0:T(8,128)(2,1)S(1)} %all_gather_reshape.3), channel_id=1, replica_groups={{0,8,16,24},{4,12,20,28},{1,9,17,25},{5,13,21,29},{2,10,18,26},{6,14,22..., dimensions={0}, use_global_device_ids=true | all-gather | bytes 983040 | tf_op jit(solution)/shard_map/all_gather | solution.py:142
  44.5 4.2 collective-permute-done.7
  59.2 6.0 collective-permute-done.3
  72.2 10.3 %shard_map.255 = (bf16[2048,256]{1,0:T(8,128)(2,1)}, bf16[2048,256]{1,0:T(8,128)(2,1)}, bf16[2048,256]{1,0:T(8,128)(2,1)}, bf16[256,2048]{1,0:T(8,128)(2,1)}, bf16[256,2048]{1,0:T(8,128)(2,1)}) custom-call(bf16[2048,768]{1,0:T(8,128)(2,1)} %pad_maximum_fusion.n_ref, bf16[768,1024]{1,0:T(8,128)(2,1)} %bitcast.239, f32[2048,256]{1,0:T(8,128)} %copy.117.c_ref, ...), custom_call_target="tpu_custom_call" | custom-call | flops 2415919104 | bytes 12582912 | tf_op jit(solution)/shard_map/pallas_call | solution.py:214
  86.1 24.7 %shard_map.256 = (bf16[2048,256]{1,0:T(8,128)(2,1)S(1)}, f32[8,2048]{1,0:T(8,128)S(1)}) custom-call(bf16[2048,256]{1,0:T(8,128)(2,1)S(1)} %copy-done.2, bf16[2048,256]{1,0:T(8,128)(2,1)S(1)} %copy-done.4, bf16[256,2048]{1,0:T(8,128)(2,1)S(1)} %copy-done.8, s32[8,2048]{1,0:T(8,128)S(1)} %pad.44.clone.rowinfo_ref, s32[2048,8]{1,0:T(8,128)S(1)} %pad_bitcast_fusion.colinfo_ref), custom_call_target="tpu_custom_call" | custom-call | flops 6442450944 | bytes 4194304 | tf_op jit(solution)/shard_map/pallas_call | solution.py:286
  112.9 2.6 copy-done.14
  123.9 3.6 fusion.38
  132.8 22.5 %collective-permute-done.5 = bf16[512,768]{1,0:T(8,128)(2,1)} collective-permute-done((bf16[512,768]{1,0:T(8,128)(2,1)}, bf16[512,768]{1,0:T(8,128)(2,1)}, u32[]{:S(2)}, u32[]{:S(2)}) %collective-permute-start.5) | collective-permute-done | bytes 786464 | tf_op jit(solution)/shard_map/ppermute | solution.py:102
  155.3 2.5 multiply_reduce_fusion.3
  176.0 10.1 %collective-permute-done.11.refs_4_ = bf16[512,896]{1,0:T(8,128)(2,1)} collective-permute-done((bf16[512,896]{1,0:T(8,128)(2,1)S(1)}, bf16[512,896]{1,0:T(8,128)(2,1)}, u32[]{:S(2)}, u32[]{:S(2)}) %collective-permute-start.11) | collective-permute-done | bytes 917536 | tf_op jit(solution)/shard_map/ppermute | solution.py:102
  189.2 4.0 collective-permute-done.21
  198.9 5.0 collective-permute-done.13
  209.2 2.8 copy.128.slot_cols_ref
  212.6 50.6 %shard_map.257 = (bf16[4,512,768]{2,1,0:T(8,128)(2,1)}, bf16[4,512,768]{2,1,0:T(8,128)(2,1)}, bf16[4,512,896]{2,1,0:T(8,128)(2,1)}, bf16[4,512,896]{2,1,0:T(8,128)(2,1)}, bf16[4,2,2,3,96,512]{5,4,3,2,1,0:T(8,128)(2,1)}) custom-call(s32[1]{0:T(128)} %bitcast.22.base_ref, s32[2,8]{1,0:T(2,128)} %pad_add_fusion.4.counts_ref, ...), custom_call_target="tpu_custom_call" | custom-call | flops 40265318400 | bytes 25165824 | tf_op jit(solution)/shard_map/pallas_call | solution.py:548
  263.3 73.3 %shard_map.258 = (bf16[4,512,768]{2,1,0:T(8,128)(2,1)}, bf16[4,512,768]{2,1,0:T(8,128)(2,1)}, bf16[4,512,896]{2,1,0:T(8,128)(2,1)}, bf16[4,512,896]{2,1,0:T(8,128)(2,1)}, bf16[4,2,2,3,96,512]{5,4,3,2,1,0:T(8,128)(2,1)}) custom-call(s32[1]{0:T(128)} %bitcast.48.base_ref, s32[2,8]{1,0:T(2,128)} %pad_add_fusion.4.counts_ref, ...), custom_call_target="tpu_custom_call" | custom-call | flops 40265318400 | bytes 25165824 | tf_op jit(solution)/shard_map/pallas_call | solution.py:548
  336.6 5.4 add_convert_fusion.2
  342.6 2.8 add_convert_fusion
  348.5 7.5 %fusion.84 = (bf16[4,512,768]{2,1,0:T(8,128)(2,1)S(1)}, f32[4,512,768]{2,1,0:T(8,128)}) fusion(bf16[4,512,768]{2,1,0:T(8,128)(2,1)} %collective-permute-done.25, bf16[4,512,768]{2,1,0:T(8,128)(2,1)} %get-tuple-element.42, bf16[4,512,768]{2,1,0:T(8,128)(2,1)} %get-tuple-element.41), kind=kLoop, calls=%fused_computation.258 | loop fusion | flops 12582912 | bytes 18874368 | tf_op jit(solution)/shard_map/convert.27
  356.9 6.9 %collective-permute-start.26 = (bf16[256,768]{1,0:T(8,128)(2,1)}, bf16[256,768]{1,0:T(8,128)(2,1)}, u32[]{:S(2)}, u32[]{:S(2)}) collective-permute-start(bf16[256,768]{1,0:T(8,128)(2,1)} %get-tuple-element.157), channel_id=1, source_target_pairs={{0,4},{4,0},{8,12},{12,8},{16,20},{20,16},{24,28},{28,24},{1,5},{5... | collective-permute-start | bytes 1179656 | tf_op jit(solution)/shard_map/ppermute | solution.py:102
  365.0 8.4 %collective-permute-done.26 = bf16[256,768]{1,0:T(8,128)(2,1)} collective-permute-done((bf16[256,768]{1,0:T(8,128)(2,1)}, bf16[256,768]{1,0:T(8,128)(2,1)}, u32[]{:S(2)}, u32[]{:S(2)}) %collective-permute-start.26) | collective-permute-done | bytes 393248 | tf_op jit(solution)/shard_map/ppermute | solution.py:102
  376.4 7.3 %fusion.83 = (bf16[4,512,896]{2,1,0:T(8,128)(2,1)}, f32[4,512,896]{2,1,0:T(8,128)S(1)}) fusion(bf16[4,512,896]{2,1,0:T(8,128)(2,1)} %collective-permute-done.30, bf16[4,512,896]{2,1,0:T(8,128)(2,1)} %get-tuple-element.46, bf16[4,512,896]{2,1,0:T(8,128)(2,1)} %get-tuple-element.45), kind=kLoop, calls=%fused_computation.257 | loop fusion | flops 14680064 | bytes 22020096 | tf_op jit(solution)/shard_map/convert.18
  383.7 2.9 slice_bitcast_fusion.10
  391.0 9.2 %collective-permute-done.31 = bf16[256,896]{1,0:T(8,128)(2,1)S(1)} collective-permute-done((bf16[256,896]{1,0:T(8,128)(2,1)S(1)}, bf16[256,896]{1,0:T(8,128)(2,1)S(1)}, u32[]{:S(2)}, u32[]{:S(2)}) %collective-permute-start.31) | collective-permute-done | bytes 458784 | tf_op jit(solution)/shard_map/ppermute | solution.py:102
  405.2 12.3 %collective-permute-done.27 = bf16[512,768]{1,0:T(8,128)(2,1)S(1)} collective-permute-done((bf16[512,768]{1,0:T(8,128)(2,1)S(1)}, bf16[512,768]{1,0:T(8,128)(2,1)S(1)}, u32[]{:S(2)}, u32[]{:S(2)}) %collective-permute-start.27) | collective-permute-done | bytes 786464 | tf_op jit(solution)/shard_map/ppermute | solution.py:102
  417.6 5.6 fusion.28
  423.7 2.7 fusion.91
  426.4 8.8 %collective-permute-done.32 = bf16[512,896]{1,0:T(8,128)(2,1)} collective-permute-done((bf16[512,896]{1,0:T(8,128)(2,1)}, bf16[512,896]{1,0:T(8,128)(2,1)}, u32[]{:S(2)}, u32[]{:S(2)}) %collective-permute-start.32) | collective-permute-done | bytes 917536 | tf_op jit(solution)/shard_map/ppermute | solution.py:102
  439.4 4.3 multiply_reduce_fusion.1
  443.8 2.8 convert_add_fusion.2
  448.9 16.8 %collective-permute-done.36 = bf16[512,768]{1,0:T(8,128)(2,1)} collective-permute-done((bf16[512,768]{1,0:T(8,128)(2,1)S(1)}, bf16[512,768]{1,0:T(8,128)(2,1)}, u32[]{:S(2)}, u32[]{:S(2)}) %collective-permute-start.36) | collective-permute-done | bytes 786464 | tf_op jit(solution)/shard_map/ppermute | solution.py:102
  465.8 4.1 fusion.79
  470.1 2.5 constant_dynamic-update-slice_fusion.13
  474.7 5.2 convolution_convert_fusion.g_ref
  479.9 53.7 %shard_map.259 = (bf16[2048,256]{1,0:T(8,128)(2,1)S(1)}, bf16[2048,256]{1,0:T(8,128)(2,1)S(1)}, bf16[2048,256]{1,0:T(8,128)(2,1)S(1)}) custom-call(bf16[2048,256]{1,0:T(8,128)(2,1)S(1)} %copy-done.3, bf16[2048,256]{1,0:T(8,128)(2,1)S(1)} %convolution_convert_fusion.g_ref, bf16[2048,256]{1,0:T(8,128)(2,1)S(1)} %get-tuple-element.40.o_ref, ...), custom_call_target="tpu_custom_call" | custom-call | flops 16106127360 | bytes 8388608 | tf_op jit(solution)/shard_map/pallas_call | solution.py:396
  537.6 6.0 fusion.85
  543.7 2.7 fusion.47
  553.4 3.4 fusion.80
  560.8 3.4 collective-permute-done.47
  564.5 29.8 %collective-permute-done.48 = f32[14736]{0:T(1024)S(1)} collective-permute-done((f32[14736]{0:T(1024)S(1)}, f32[14736]{0:T(1024)S(1)}, u32[]{:S(2)}, u32[]{:S(2)}) %collective-permute-start.48) | collective-permute-done | bytes 58976 | tf_op jit(solution)/shard_map/ppermute | solution.py:102
  596.6 2.6 collective-permute-done.41
  600.2 2.7 collective-permute-done.42
  604.8 2.9 collective-permute-start.50
  607.7 3.4 collective-permute-start.44
  622.9 2.7 fusion.31
  631.2 3.4 reduce-scatter.8.cloned.1.call-done
  637.3 4.3 collective-permute-done.39
  644.0 3.1 fusion.12
  (403 shorter events, 153.0 us)
Async XLA Ops:
  7.2 205.4 %all-gather.5.cloned.1.call-start = ((), (), s32[]{:S(2)}) async-start(), calls=%async_computation.6 | async-start | bytes 5898240 | tf_op jit(solution)/shard_map/all_gather | solution.py:142
  10.9 43.2 %collective-permute-start.1 = (bf16[512,768]{1,0:T(8,128)(2,1)}, bf16[512,768]{1,0:T(8,128)(2,1)}, u32[]{:S(2)}, u32[]{:S(2)}) collective-permute-start(bf16[512,768]{1,0:T(8,128)(2,1)} %fusion.26), channel_id=1, source_target_pairs={{0,2},{1,3},{2,0},{3,1},{4,6},{5,7},{6,4},{7,5},{8,10},{9,11},{10,... | collective-permute-start | bytes 2359304 | tf_op jit(solution)/shard_map/ppermute | solution.py:102
  13.8 54.4 %collective-permute-start = (bf16[512,768]{1,0:T(8,128)(2,1)}, bf16[512,768]{1,0:T(8,128)(2,1)}, u32[]{:S(2)}, u32[]{:S(2)}) collective-permute-start(bf16[512,768]{1,0:T(8,128)(2,1)} %fusion.26), channel_id=1, source_target_pairs={{0,1},{1,0},{2,3},{3,2},{4,5},{5,4},{6,7},{7,6},{8,9},{9,8},{10,11... | collective-permute-start | bytes 2359304 | tf_op jit(solution)/shard_map/ppermute | solution.py:102
  19.7 24.8 %collective-permute-start.24 = (bf16[2,3,96,512]{3,2,1,0:T(8,128)(2,1)}, bf16[2,3,96,512]{3,2,1,0:T(8,128)(2,1)S(1)}, u32[]{:S(2)}, u32[]{:S(2)}) collective-permute-start(bf16[2,3,96,512]{3,2,1,0:T(8,128)(2,1)} %get-tuple-element.176), channel_id=1, source_target_pairs={{0,4},{4,0},{8,12},{12,8},{16,20},{20,16},{24,28},{28,24},{1,5},{5... | collective-permute-start | bytes 1769480 | tf_op jit(solution)/shard_map/ppermute | solution.py:102
  21.2 27.5 %collective-permute-start.7 = (bf16[2,3,96,512]{3,2,1,0:T(8,128)(2,1)}, bf16[2,3,96,512]{3,2,1,0:T(8,128)(2,1)S(1)}, u32[]{:S(2)}, u32[]{:S(2)}) collective-permute-start(bf16[2,3,96,512]{3,2,1,0:T(8,128)(2,1)} %get-tuple-element.175), channel_id=1, source_target_pairs={{0,4},{4,0},{8,12},{12,8},{16,20},{20,16},{24,28},{28,24},{1,5},{5... | collective-permute-start | bytes 1769480 | tf_op jit(solution)/shard_map/ppermute | solution.py:102
  42.5 22.7 %collective-permute-start.3 = (bf16[4,96,1024]{2,1,0:T(8,128)(2,1)}, bf16[4,96,1024]{2,1,0:T(8,128)(2,1)}, u32[]{:S(2)}, u32[]{:S(2)}) collective-permute-start(bf16[4,96,1024]{2,1,0:T(8,128)(2,1)} %all_gather.15), channel_id=1, source_target_pairs={{0,4},{4,0},{8,12},{12,8},{16,20},{20,16},{24,28},{28,24},{1,5},{5... | collective-permute-start | bytes 2359304 | tf_op jit(solution)/shard_map/ppermute | solution.py:102
  52.9 210.5 %all-gather.7.cloned.1.call-start = ((), (), s32[]{:S(2)}) async-start(), calls=%async_computation.7 | async-start | bytes 5898240 | tf_op jit(solution)/shard_map/all_gather | solution.py:142
  54.1 14.1 %collective-permute-start.2 = (bf16[512,768]{1,0:T(8,128)(2,1)}, bf16[512,768]{1,0:T(8,128)(2,1)}, u32[]{:S(2)}, u32[]{:S(2)}) collective-permute-start(bf16[512,768]{1,0:T(8,128)(2,1)} %collective-permute-done.1), channel_id=1, source_target_pairs={{0,1},{1,0},{2,3},{3,2},{4,5},{5,4},{6,7},{7,6},{8,9},{9,8},{10,11... | collective-permute-start | bytes 2359304 | tf_op jit(solution)/shard_map/ppermute | solution.py:102
  116.9 48.1 %collective-permute-start.19 = (bf16[512,768]{1,0:T(8,128)(2,1)}, bf16[512,768]{1,0:T(8,128)(2,1)}, u32[]{:S(2)}, u32[]{:S(2)}) collective-permute-start(bf16[512,768]{1,0:T(8,128)(2,1)} %refs_8_.3), channel_id=1, source_target_pairs={{0,4},{4,0},{8,12},{12,8},{16,20},{20,16},{24,28},{28,24},{1,5},{5... | collective-permute-start | bytes 2359304 | tf_op jit(solution)/shard_map/ppermute | solution.py:102
  118.4 49.9 %collective-permute-start.17 = (bf16[512,768]{1,0:T(8,128)(2,1)}, bf16[512,768]{1,0:T(8,128)(2,1)}, u32[]{:S(2)}, u32[]{:S(2)}) collective-permute-start(bf16[512,768]{1,0:T(8,128)(2,1)} %refs_8_.3), channel_id=1, source_target_pairs={{0,2},{1,3},{2,0},{3,1},{4,6},{5,7},{6,4},{7,5},{8,10},{9,11},{10,... | collective-permute-start | bytes 2359304 | tf_op jit(solution)/shard_map/ppermute | solution.py:102
  119.0 53.9 %collective-permute-start.6 = (s32[2048,2]{0,1:T(2,128)S(1)}, s32[2048,2]{0,1:T(2,128)}, u32[]{:S(2)}, u32[]{:S(2)}) collective-permute-start(s32[2048,2]{0,1:T(2,128)S(1)} %copy-done.50), channel_id=1, source_target_pairs={{0,4},{4,0},{8,12},{12,8},{16,20},{20,16},{24,28},{28,24},{1,5},{5... | collective-permute-start | bytes 49160 | tf_op jit(solution)/shard_map/ppermute | solution.py:102
  127.6 27.7 %collective-permute-start.5 = (bf16[512,768]{1,0:T(8,128)(2,1)}, bf16[512,768]{1,0:T(8,128)(2,1)}, u32[]{:S(2)}, u32[]{:S(2)}) collective-permute-start(bf16[512,768]{1,0:T(8,128)(2,1)} %fusion.38), channel_id=1, source_target_pairs={{0,2},{1,3},{2,0},{3,1},{4,6},{5,7},{6,4},{7,5},{8,10},{9,11},{10,... | collective-permute-start | bytes 2359304 | tf_op jit(solution)/shard_map/ppermute | solution.py:102
  132.5 314.1 %reduce-scatter.4.cloned.1.call-start = ((), (), s32[]{:S(2)}) async-start(), calls=%async_computation.3 | async-start | bytes 5898240 | tf_op jit(solution)/shard_map/reduce_scatter | solution.py:146
  162.7 23.5 %collective-permute-start.11 = (bf16[512,896]{1,0:T(8,128)(2,1)S(1)}, bf16[512,896]{1,0:T(8,128)(2,1)}, u32[]{:S(2)}, u32[]{:S(2)}) collective-permute-start(bf16[512,896]{1,0:T(8,128)(2,1)S(1)} %fusion.49.refs_0_), channel_id=1, source_target_pairs={{0,4},{4,0},{8,12},{12,8},{16,20},{20,16},{24,28},{28,24},{1,5},{5... | collective-permute-start | bytes 2752520 | tf_op jit(solution)/shard_map/ppermute | solution.py:102
  163.3 23.4 %collective-permute-start.9 = (bf16[512,896]{1,0:T(8,128)(2,1)S(1)}, bf16[512,896]{1,0:T(8,128)(2,1)}, u32[]{:S(2)}, u32[]{:S(2)}) collective-permute-start(bf16[512,896]{1,0:T(8,128)(2,1)S(1)} %fusion.49.refs_0_), channel_id=1, source_target_pairs={{0,2},{1,3},{2,0},{3,1},{4,6},{5,7},{6,4},{7,5},{8,10},{9,11},{10,... | collective-permute-start | bytes 2752520 | tf_op jit(solution)/shard_map/ppermute | solution.py:102
  166.8 26.4 %collective-permute-start.21 = (bf16[256,768]{1,0:T(8,128)(2,1)}, bf16[256,768]{1,0:T(8,128)(2,1)}, u32[]{:S(2)}, u32[]{:S(2)}) collective-permute-start(bf16[256,768]{1,0:T(8,128)(2,1)} %slice.345), channel_id=1, source_target_pairs={{0,2},{1,3},{2,0},{3,1},{4,6},{5,7},{6,4},{7,5},{8,10},{9,11},{10,... | collective-permute-start | bytes 1179656 | tf_op jit(solution)/shard_map/ppermute | solution.py:102
  170.1 23.8 %collective-permute-start.22 = (bf16[256,768]{1,0:T(8,128)(2,1)}, bf16[256,768]{1,0:T(8,128)(2,1)}, u32[]{:S(2)}, u32[]{:S(2)}) collective-permute-start(bf16[256,768]{1,0:T(8,128)(2,1)} %slice.346), channel_id=1, source_target_pairs={{0,4},{4,0},{8,12},{12,8},{16,20},{20,16},{24,28},{28,24},{1,5},{5... | collective-permute-start | bytes 1179656 | tf_op jit(solution)/shard_map/ppermute | solution.py:102
  172.8 33.3 %collective-permute-start.16 = (bf16[512,768]{1,0:T(8,128)(2,1)}, bf16[512,768]{1,0:T(8,128)(2,1)}, u32[]{:S(2)}, u32[]{:S(2)}) collective-permute-start(bf16[512,768]{1,0:T(8,128)(2,1)} %refs_8_.3), channel_id=1, source_target_pairs={{0,1},{1,0},{2,3},{3,2},{4,5},{5,4},{6,7},{7,6},{8,9},{9,8},{10,11... | collective-permute-start | bytes 2359304 | tf_op jit(solution)/shard_map/ppermute | solution.py:102
  186.1 20.0 %collective-permute-start.18 = (bf16[512,768]{1,0:T(8,128)(2,1)}, bf16[512,768]{1,0:T(8,128)(2,1)}, u32[]{:S(2)}, u32[]{:S(2)}) collective-permute-start(bf16[512,768]{1,0:T(8,128)(2,1)} %collective-permute-done.17.refs_10_), channel_id=1, source_target_pairs={{0,1},{1,0},{2,3},{3,2},{4,5},{5,4},{6,7},{7,6},{8,9},{9,8},{10,11... | collective-permute-start | bytes 2359304 | tf_op jit(solution)/shard_map/ppermute | solution.py:102
  186.6 20.0 %collective-permute-start.20 = (bf16[512,768]{1,0:T(8,128)(2,1)}, bf16[512,768]{1,0:T(8,128)(2,1)}, u32[]{:S(2)}, u32[]{:S(2)}) collective-permute-start(bf16[512,768]{1,0:T(8,128)(2,1)} %collective-permute-done.19.refs_12_), channel_id=1, source_target_pairs={{0,1},{1,0},{2,3},{3,2},{4,5},{5,4},{6,7},{7,6},{8,9},{9,8},{10,11... | collective-permute-start | bytes 2359304 | tf_op jit(solution)/shard_map/ppermute | solution.py:102
  193.2 10.7 %collective-permute-start.13 = (bf16[256,896]{1,0:T(8,128)(2,1)S(1)}, bf16[256,896]{1,0:T(8,128)(2,1)S(1)}, u32[]{:S(2)}, u32[]{:S(2)}) collective-permute-start(bf16[256,896]{1,0:T(8,128)(2,1)S(1)} %slice.343), channel_id=1, source_target_pairs={{0,2},{1,3},{2,0},{3,1},{4,6},{5,7},{6,4},{7,5},{8,10},{9,11},{10,... | collective-permute-start | bytes 1376264 | tf_op jit(solution)/shard_map/ppermute | solution.py:102
  193.9 10.8 %collective-permute-start.14 = (bf16[256,896]{1,0:T(8,128)(2,1)S(1)}, bf16[256,896]{1,0:T(8,128)(2,1)S(1)}, u32[]{:S(2)}, u32[]{:S(2)}) collective-permute-start(bf16[256,896]{1,0:T(8,128)(2,1)S(1)} %slice.344), channel_id=1, source_target_pairs={{0,4},{4,0},{8,12},{12,8},{16,20},{20,16},{24,28},{28,24},{1,5},{5... | collective-permute-start | bytes 1376264 | tf_op jit(solution)/shard_map/ppermute | solution.py:102
  203.9 8.7 %collective-permute-start.23 = (bf16[512,768]{1,0:T(8,128)(2,1)}, bf16[512,768]{1,0:T(8,128)(2,1)}, u32[]{:S(2)}, u32[]{:S(2)}) collective-permute-start(bf16[512,768]{1,0:T(8,128)(2,1)} %constant_dynamic-update-slice_fusion.10.refs_14_), channel_id=1, source_target_pairs={{0,1},{1,0},{2,3},{3,2},{4,5},{5,4},{6,7},{7,6},{8,9},{9,8},{10,11... | collective-permute-start | bytes 2359304 | tf_op jit(solution)/shard_map/ppermute | solution.py:102
  204.7 7.9 %collective-permute-start.8 = (bf16[512,896]{1,0:T(8,128)(2,1)S(1)}, bf16[512,896]{1,0:T(8,128)(2,1)}, u32[]{:S(2)}, u32[]{:S(2)}) collective-permute-start(bf16[512,896]{1,0:T(8,128)(2,1)S(1)} %fusion.49.refs_0_), channel_id=1, source_target_pairs={{0,1},{1,0},{2,3},{3,2},{4,5},{5,4},{6,7},{7,6},{8,9},{9,8},{10,11... | collective-permute-start | bytes 2752520 | tf_op jit(solution)/shard_map/ppermute | solution.py:102
  206.1 6.5 collective-permute-start.10
  206.1 6.4 collective-permute-start.12
  263.2 274.3 %reduce-scatter.6.cloned.1.call-start = ((), (), s32[]{:S(2)}) async-start(), calls=%async_computation.4 | async-start | bytes 5898240 | tf_op jit(solution)/shard_map/reduce_scatter | solution.py:146
  345.3 31.1 %collective-permute-start.30 = (bf16[4,512,896]{2,1,0:T(8,128)(2,1)}, bf16[4,512,896]{2,1,0:T(8,128)(2,1)}, u32[]{:S(2)}, u32[]{:S(2)}) collective-permute-start(bf16[4,512,896]{2,1,0:T(8,128)(2,1)} %add_convert_fusion), channel_id=1, source_target_pairs={{0,1},{1,0},{2,3},{3,2},{4,5},{5,4},{6,7},{7,6},{8,9},{9,8},{10,11... | collective-permute-start | bytes 11010056 | tf_op jit(solution)/shard_map/ppermute | solution.py:102
  356.9 16.5 %collective-permute-start.26 = (bf16[256,768]{1,0:T(8,128)(2,1)}, bf16[256,768]{1,0:T(8,128)(2,1)}, u32[]{:S(2)}, u32[]{:S(2)}) collective-permute-start(bf16[256,768]{1,0:T(8,128)(2,1)} %get-tuple-element.157), channel_id=1, source_target_pairs={{0,4},{4,0},{8,12},{12,8},{16,20},{20,16},{24,28},{28,24},{1,5},{5... | collective-permute-start | bytes 1179656 | tf_op jit(solution)/shard_map/ppermute | solution.py:102
  363.7 10.9 %collective-permute-start.28 = (bf16[256,768]{1,0:T(8,128)(2,1)S(1)}, bf16[256,768]{1,0:T(8,128)(2,1)}, u32[]{:S(2)}, u32[]{:S(2)}) collective-permute-start(bf16[256,768]{1,0:T(8,128)(2,1)S(1)} %get-tuple-element.156), channel_id=1, source_target_pairs={{0,2},{1,3},{2,0},{3,1},{4,6},{5,7},{6,4},{7,5},{8,10},{9,11},{10,... | collective-permute-start | bytes 1179656 | tf_op jit(solution)/shard_map/ppermute | solution.py:102
  365.0 269.6 %reduce-scatter.8.cloned.1.call-start = ((), (), s32[]{:S(2)}) async-start(), calls=%async_computation.5 | async-start | bytes 983040 | tf_op jit(solution)/shard_map/reduce_scatter | solution.py:146
  386.7 13.5 %collective-permute-start.31 = (bf16[256,896]{1,0:T(8,128)(2,1)S(1)}, bf16[256,896]{1,0:T(8,128)(2,1)S(1)}, u32[]{:S(2)}, u32[]{:S(2)}) collective-permute-start(bf16[256,896]{1,0:T(8,128)(2,1)S(1)} %get-tuple-element.147), channel_id=1, source_target_pairs={{0,4},{4,0},{8,12},{12,8},{16,20},{20,16},{24,28},{28,24},{1,5},{5... | collective-permute-start | bytes 1376264 | tf_op jit(solution)/shard_map/ppermute | solution.py:102
  387.2 13.5 %collective-permute-start.33 = (bf16[256,896]{1,0:T(8,128)(2,1)S(1)}, bf16[256,896]{1,0:T(8,128)(2,1)S(1)}, u32[]{:S(2)}, u32[]{:S(2)}) collective-permute-start(bf16[256,896]{1,0:T(8,128)(2,1)S(1)} %get-tuple-element.146), channel_id=1, source_target_pairs={{0,2},{1,3},{2,0},{3,1},{4,6},{5,7},{6,4},{7,5},{8,10},{9,11},{10,... | collective-permute-start | bytes 1376264 | tf_op jit(solution)/shard_map/ppermute | solution.py:102
  387.9 29.6 %collective-permute-start.27 = (bf16[512,768]{1,0:T(8,128)(2,1)S(1)}, bf16[512,768]{1,0:T(8,128)(2,1)S(1)}, u32[]{:S(2)}, u32[]{:S(2)}) collective-permute-start(bf16[512,768]{1,0:T(8,128)(2,1)S(1)} %pad_maximum_fusion.10), channel_id=1, source_target_pairs={{0,2},{1,3},{2,0},{3,1},{4,6},{5,7},{6,4},{7,5},{8,10},{9,11},{10,... | collective-permute-start | bytes 2359304 | tf_op jit(solution)/shard_map/ppermute | solution.py:102
  389.4 28.1 %collective-permute-start.29 = (bf16[512,768]{1,0:T(8,128)(2,1)S(1)}, bf16[512,768]{1,0:T(8,128)(2,1)S(1)}, u32[]{:S(2)}, u32[]{:S(2)}) collective-permute-start(bf16[512,768]{1,0:T(8,128)(2,1)S(1)} %pad_maximum_fusion.11), channel_id=1, source_target_pairs={{0,4},{4,0},{8,12},{12,8},{16,20},{20,16},{24,28},{28,24},{1,5},{5... | collective-permute-start | bytes 2359304 | tf_op jit(solution)/shard_map/ppermute | solution.py:102
  402.0 33.3 %collective-permute-start.32 = (bf16[512,896]{1,0:T(8,128)(2,1)}, bf16[512,896]{1,0:T(8,128)(2,1)}, u32[]{:S(2)}, u32[]{:S(2)}) collective-permute-start(bf16[512,896]{1,0:T(8,128)(2,1)} %pad_maximum_fusion.8), channel_id=1, source_target_pairs={{0,2},{1,3},{2,0},{3,1},{4,6},{5,7},{6,4},{7,5},{8,10},{9,11},{10,... | collective-permute-start | bytes 2752520 | tf_op jit(solution)/shard_map/ppermute | solution.py:102
  403.7 31.6 %collective-permute-start.34 = (bf16[512,896]{1,0:T(8,128)(2,1)}, bf16[512,896]{1,0:T(8,128)(2,1)}, u32[]{:S(2)}, u32[]{:S(2)}) collective-permute-start(bf16[512,896]{1,0:T(8,128)(2,1)} %pad_maximum_fusion.9), channel_id=1, source_target_pairs={{0,4},{4,0},{8,12},{12,8},{16,20},{20,16},{24,28},{28,24},{1,5},{5... | collective-permute-start | bytes 2752520 | tf_op jit(solution)/shard_map/ppermute | solution.py:102
  448.1 17.7 %collective-permute-start.36 = (bf16[512,768]{1,0:T(8,128)(2,1)S(1)}, bf16[512,768]{1,0:T(8,128)(2,1)}, u32[]{:S(2)}, u32[]{:S(2)}) collective-permute-start(bf16[512,768]{1,0:T(8,128)(2,1)S(1)} %convert_element_type.209), channel_id=1, source_target_pairs={{0,2},{1,3},{2,0},{3,1},{4,6},{5,7},{6,4},{7,5},{8,10},{9,11},{10,... | collective-permute-start | bytes 2359304 | tf_op jit(solution)/shard_map/ppermute | solution.py:102
  448.9 23.7 %collective-permute-start.35 = (bf16[512,768]{1,0:T(8,128)(2,1)S(1)}, bf16[512,768]{1,0:T(8,128)(2,1)}, u32[]{:S(2)}, u32[]{:S(2)}) collective-permute-start(bf16[512,768]{1,0:T(8,128)(2,1)S(1)} %convert_element_type.209), channel_id=1, source_target_pairs={{0,1},{1,0},{2,3},{3,2},{4,5},{5,4},{6,7},{7,6},{8,9},{9,8},{10,11... | collective-permute-start | bytes 2359304 | tf_op jit(solution)/shard_map/ppermute | solution.py:102
  465.7 6.9 %collective-permute-start.37 = (bf16[512,768]{1,0:T(8,128)(2,1)}, bf16[512,768]{1,0:T(8,128)(2,1)}, u32[]{:S(2)}, u32[]{:S(2)}) collective-permute-start(bf16[512,768]{1,0:T(8,128)(2,1)} %collective-permute-done.36), channel_id=1, source_target_pairs={{0,1},{1,0},{2,3},{3,2},{4,5},{5,4},{6,7},{7,6},{8,9},{9,8},{10,11... | collective-permute-start | bytes 2359304 | tf_op jit(solution)/shard_map/ppermute | solution.py:102
  547.6 71.7 %collective-permute-start.51 = (bf16[4,3,96,512]{3,2,1,0:T(8,128)(2,1)}, bf16[4,3,96,512]{3,2,1,0:T(8,128)(2,1)}, u32[]{:S(2)}, u32[]{:S(2)}) collective-permute-start(bf16[4,3,96,512]{3,2,1,0:T(8,128)(2,1)} %dynamic-slice_bitcast_fusion), channel_id=1, source_target_pairs={{0,4},{4,0},{8,12},{12,8},{16,20},{20,16},{24,28},{28,24},{1,5},{5... | collective-permute-start | bytes 3538952 | tf_op jit(solution)/shard_map/ppermute | solution.py:102
  549.5 61.7 %collective-permute-start.45 = (bf16[4,96,1024]{2,1,0:T(8,128)(2,1)}, bf16[4,96,1024]{2,1,0:T(8,128)(2,1)}, u32[]{:S(2)}, u32[]{:S(2)}) collective-permute-start(bf16[4,96,1024]{2,1,0:T(8,128)(2,1)} %fusion.55), channel_id=1, source_target_pairs={{0,4},{4,0},{8,12},{12,8},{16,20},{20,16},{24,28},{28,24},{1,5},{5... | collective-permute-start | bytes 2359304 | tf_op jit(solution)/shard_map/ppermute | solution.py:102
  552.7 68.5 %collective-permute-start.38 = (bf16[1024,768]{1,0:T(8,128)(2,1)}, bf16[1024,768]{1,0:T(8,128)(2,1)}, u32[]{:S(2)}, u32[]{:S(2)}) collective-permute-start(bf16[1024,768]{1,0:T(8,128)(2,1)} %pad_maximum_fusion.5), channel_id=1, source_target_pairs={{0,1},{1,0},{2,3},{3,2},{4,5},{5,4},{6,7},{7,6},{8,9},{9,8},{10,11... | collective-permute-start | bytes 4718600 | tf_op jit(solution)/shard_map/ppermute | solution.py:102
  564.2 30.1 %collective-permute-start.48 = (f32[14736]{0:T(1024)S(1)}, f32[14736]{0:T(1024)S(1)}, u32[]{:S(2)}, u32[]{:S(2)}) collective-permute-start(f32[14736]{0:T(1024)S(1)} %add.305), channel_id=1, source_target_pairs={{0,4},{4,0},{8,12},{12,8},{16,20},{20,16},{24,28},{28,24},{1,5},{5... | collective-permute-start | bytes 176840 | tf_op jit(solution)/shard_map/ppermute | solution.py:102
  594.3 10.5 %collective-permute-start.49 = (f32[14736]{0:T(1024)S(1)}, f32[14736]{0:T(1024)S(1)}, u32[]{:S(2)}, u32[]{:S(2)}) collective-permute-start(f32[14736]{0:T(1024)S(1)} %add.306), channel_id=1, source_target_pairs={{0,8},{4,12},{8,0},{12,4},{16,24},{20,28},{24,16},{28,20},{1,9},{5... | collective-permute-start | bytes 176840 | tf_op jit(solution)/shard_map/ppermute | solution.py:102
  604.8 9.4 %collective-permute-start.50 = (f32[14736]{0:T(1024)S(1)}, f32[14736]{0:T(1024)S(1)}, u32[]{:S(2)}, u32[]{:S(2)}) collective-permute-start(f32[14736]{0:T(1024)S(1)} %add.307), channel_id=1, source_target_pairs={{0,16},{4,20},{8,24},{12,28},{16,0},{20,4},{24,8},{28,12},{1,17},{... | collective-permute-start | bytes 176840 | tf_op jit(solution)/shard_map/ppermute | solution.py:102
  607.7 10.9 %collective-permute-start.44 = (f32[768]{0:T(1024)S(1)}, f32[768]{0:T(1024)S(1)}, u32[]{:S(2)}, u32[]{:S(2)}) collective-permute-start(f32[768]{0:T(1024)S(1)} %add.299), channel_id=1, source_target_pairs={{0,16},{4,20},{8,24},{12,28},{16,0},{20,4},{24,8},{28,12},{1,17},{... | collective-permute-start | bytes 9224 | tf_op jit(solution)/shard_map/ppermute | solution.py:102
  625.7 16.0 %collective-permute-start.39 = (bf16[512,768]{1,0:T(8,128)(2,1)S(1)}, bf16[512,768]{1,0:T(8,128)(2,1)S(1)}, u32[]{:S(2)}, u32[]{:S(2)}) collective-permute-start(bf16[512,768]{1,0:T(8,128)(2,1)S(1)} %fusion.31), channel_id=1, source_target_pairs={{0,2},{1,3},{2,0},{3,1},{4,6},{5,7},{6,4},{7,5},{8,10},{9,11},{10,... | collective-permute-start | bytes 2359304 | tf_op jit(solution)/shard_map/ppermute | solution.py:102
  (74 other events, 768.8 us)
Sparse Core Ops, SparseCore 0:
  53.0 89.7 all-gather.4
  144.3 87.8 all-gather.6
  263.4 94.5 reduce-scatter.3
  365.1 85.1 reduce-scatter.5
  613.6 20.9 reduce-scatter.7
